TPU v7x, 128 devices: a whole 4x4x4 slice. The times are simulated.
128 devices in a mesh: ctx: 32 (over x, y_lo, z), sub: 4 (over y_hi, core).
Axes of the slice: x: 4, y: 4 (y_hi: 2, y_lo: 2; y = y_hi * 2 + y_lo), z: 4, core: 2. Of those that a mesh axis runs over, the one named last changes fastest.
Arguments:
- queries: bfloat16 [128, 65536], P(None, ('ctx', 'sub')), may hold values from -6 to 6
- key_branch: bfloat16 [128, 65536], P(None, ('ctx', 'sub')), may hold values from -6 to 6
- value_branch: bfloat16 [128, 65536], P(None, ('ctx', 'sub')), may hold values from -6 to 6
- out_grad: bfloat16 [128, 65536], P(None, ('ctx', 'sub')), as said below
- residue: float32 [128, 16], P(('ctx', 'sub')), as said below
- log_rate: float32 [128, 16], P(('ctx', 'sub')), as said below
- skip_gain: float32 [128], replicated, may hold values from 0.5 to 1.5
Outputs:
- output: bfloat16 [128, 65536], P(None, ('ctx', 'sub'))
- grad_query: bfloat16 [128, 65536], P(None, ('ctx', 'sub'))
- grad_key: bfloat16 [128, 65536], P(None, ('ctx', 'sub'))
- grad_value: bfloat16 [128, 65536], P(None, ('ctx', 'sub'))
- grad_residue: float32 [128, 16], P(('ctx', 'sub'))
- grad_log_rate: float32 [128, 16], P(('ctx', 'sub'))
- grad_skip: float32 [128], P(('ctx', 'sub'))
Inputs may be any that keep to these rules, and one draw needn't show every extreme that they name: `out_grad`: each entry lies between -18 and 18. exp(log_rate) lies between 0.2 / 65536 and 0.1. `residue`: real-valued residues.
All inputs are finite; a program needn't handle non-finite values.
Results may differ from a plain program's by a relative error of at most 0.027.
Values may be sent and summed in bfloat16 or wider, within the bound.
A program may use at most 128 MiB of HBM per device.

v0:
```python
import math

import jax
import jax.numpy as jnp
from jax import lax
from jax.sharding import PartitionSpec as P

FULL_PRECISION = lax.Precision.HIGHEST


def counting(length):
    return jnp.arange(length, dtype=jnp.int32)


def phases(first_ids, second_ids, period):
    product = first_ids[:, None] * second_ids[None, :] % period
    angles = product.astype(jnp.float32) * (2.0 * math.pi / period)
    return (jnp.cos(angles), jnp.sin(angles))


def across_forward(values, freq_rows):
    sources = values.shape[-2]
    cosine, sine = phases(counting(freq_rows), counting(sources), freq_rows)
    values = values.astype(jnp.float32)
    real_part = jnp.einsum("ka,...ab->...kb", cosine, values, precision=FULL_PRECISION)
    imag_part = -jnp.einsum("ka,...ab->...kb", sine, values, precision=FULL_PRECISION)
    return (real_part, imag_part)


def across_inverse(real_part, imag_part, sources):
    freq_rows = real_part.shape[-2]
    period_len = freq_rows * real_part.shape[-1]
    cosine, sine = phases(counting(sources), counting(freq_rows), freq_rows)
    combined = jnp.einsum("ak,...kb->...ab", cosine, real_part, precision=FULL_PRECISION)
    combined = combined - jnp.einsum("ak,...kb->...ab", sine, imag_part, precision=FULL_PRECISION)
    return combined / period_len


def twist(real_part, imag_part, sign):
    freq_rows, tok_width = (real_part.shape[-2], real_part.shape[-1])
    cosine, sine = phases(counting(freq_rows), counting(tok_width), freq_rows * tok_width)
    sine = sign * sine
    return (real_part * cosine - imag_part * sine, real_part * sine + imag_part * cosine)


def split_width(tok_width):
    inner_len = min(128, tok_width)
    return (tok_width // inner_len, inner_len)


def left_product(mat_real, mat_imag, real_part, imag_part):

    def contract(matrix, values):
        return jnp.einsum("pq,...qb->...pb", matrix, values, precision=FULL_PRECISION)

    return (
        contract(mat_real, real_part) - contract(mat_imag, imag_part),
        contract(mat_real, imag_part) + contract(mat_imag, real_part),
    )


def right_product(real_part, imag_part, mat_real, mat_imag):

    def contract(values, matrix):
        return jnp.einsum("...bq,qp->...bp", values, matrix, precision=FULL_PRECISION)

    return (
        contract(real_part, mat_real) - contract(imag_part, mat_imag),
        contract(real_part, mat_imag) + contract(imag_part, mat_real),
    )


def local_tables(tok_width):
    outer_len, inner_len = split_width(tok_width)
    cos_outer, sin_outer = phases(counting(outer_len), counting(outer_len), outer_len)
    cos_mid, sin_mid = phases(counting(outer_len), counting(inner_len), tok_width)
    cos_inner, sin_inner = phases(counting(inner_len), counting(inner_len), inner_len)
    return (outer_len, inner_len, cos_outer, sin_outer, cos_mid, sin_mid, cos_inner, sin_inner)


def local_forward(real_part, imag_part):
    flat_shape = real_part.shape
    outer_len, inner_len, cos_outer, sin_outer, cos_mid, sin_mid, cos_inner, sin_inner = (
        local_tables(flat_shape[-1])
    )
    grid_shape = flat_shape[:-1] + (outer_len, inner_len)
    real_part = real_part.reshape(grid_shape)
    imag_part = imag_part.reshape(grid_shape)
    real_part, imag_part = left_product(cos_outer, -sin_outer, real_part, imag_part)
    real_part, imag_part = (
        real_part * cos_mid + imag_part * sin_mid,
        imag_part * cos_mid - real_part * sin_mid,
    )
    real_part, imag_part = right_product(real_part, imag_part, cos_inner, -sin_inner)
    return (real_part.reshape(flat_shape), imag_part.reshape(flat_shape))


def local_inverse(real_part, imag_part):
    flat_shape = real_part.shape
    outer_len, inner_len, cos_outer, sin_outer, cos_mid, sin_mid, cos_inner, sin_inner = (
        local_tables(flat_shape[-1])
    )
    grid_shape = flat_shape[:-1] + (outer_len, inner_len)
    real_part = real_part.reshape(grid_shape)
    imag_part = imag_part.reshape(grid_shape)
    real_part, imag_part = right_product(real_part, imag_part, cos_inner, sin_inner)
    real_part, imag_part = (
        real_part * cos_mid - imag_part * sin_mid,
        imag_part * cos_mid + real_part * sin_mid,
    )
    real_part, imag_part = left_product(cos_outer, sin_outer, real_part, imag_part)
    return (real_part.reshape(flat_shape), imag_part.reshape(flat_shape))


def build_filter(residue, log_rate, seq_len):
    positions = counting(seq_len).astype(jnp.float32)
    decay_rate = jnp.exp(log_rate)

    def add_mode(mode_idx, total):
        weight = lax.dynamic_slice_in_dim(residue, mode_idx, 1, 1)
        speed = lax.dynamic_slice_in_dim(decay_rate, mode_idx, 1, 1)
        return total + weight * jnp.exp(-speed * positions[None, :])

    start_total = jnp.zeros((residue.shape[0], seq_len), jnp.float32)
    return lax.fori_loop(0, residue.shape[1], add_mode, start_total)


def filter_grads(lag_grad, residue, log_rate):
    seq_len = lag_grad.shape[1]
    positions = counting(seq_len).astype(jnp.float32)
    decay_rate = jnp.exp(log_rate)

    def one_mode(mode_idx, sums):
        plain_sums, timed_sums = sums
        speed = lax.dynamic_slice_in_dim(decay_rate, mode_idx, 1, 1)
        weighted = lag_grad * jnp.exp(-speed * positions[None, :])
        plain_sums = lax.dynamic_update_slice_in_dim(
            plain_sums, jnp.sum(weighted, axis=1, keepdims=True), mode_idx, 1
        )
        timed_sums = lax.dynamic_update_slice_in_dim(
            timed_sums, jnp.sum(weighted * positions[None, :], axis=1, keepdims=True), mode_idx, 1
        )
        return (plain_sums, timed_sums)

    empty_sums = jnp.zeros_like(residue)
    plain_sums, timed_sums = lax.fori_loop(0, residue.shape[1], one_mode, (empty_sums, empty_sums))
    return (plain_sums / seq_len, -residue * decay_rate * timed_sums / math.sqrt(seq_len))


def body(queries, key_branch, value_branch, out_grad, residue, log_rate, skip_gain):
    devices = lax.axis_size(("ctx", "sub"))
    channels, tok_width = queries.shape
    local_chans = channels // devices
    freq_rows = 2 * devices
    seq_len = devices * tok_width
    mixed = (key_branch.astype(jnp.float32) * value_branch.astype(jnp.float32)).astype(jnp.bfloat16)
    gated = (out_grad.astype(jnp.float32) * queries.astype(jnp.float32)).astype(jnp.bfloat16)
    paired = jnp.stack([mixed, gated])
    real_part, imag_part = across_forward(
        lax.all_to_all(
            paired[:, :, None, :], ("ctx", "sub"), split_axis=1, concat_axis=2, tiled=True
        ),
        freq_rows,
    )
    spec_real, spec_imag = local_forward(*twist(real_part, imag_part, -1.0))
    filt = build_filter(residue, log_rate, seq_len).reshape(local_chans, devices, tok_width)
    filt_real, filt_imag = local_forward(*twist(*across_forward(filt, freq_rows), -1.0))
    in_real, in_imag = (spec_real[0], spec_imag[0])
    gr_real, gr_imag = (spec_real[1], spec_imag[1])
    prod_real = jnp.stack(
        [
            in_real * filt_real - in_imag * filt_imag,
            filt_real * gr_real + filt_imag * gr_imag,
            in_real * gr_real + in_imag * gr_imag,
        ]
    )
    prod_imag = jnp.stack(
        [
            in_real * filt_imag + in_imag * filt_real,
            filt_real * gr_imag - filt_imag * gr_real,
            in_real * gr_imag - in_imag * gr_real,
        ]
    )
    results = across_inverse(*twist(*local_inverse(prod_real, prod_imag), 1.0), devices)
    lag_grad = results[2].reshape(local_chans, seq_len)
    grad_residue, grad_log_rate = filter_grads(lag_grad, residue, log_rate)
    back = lax.all_to_all(results[:2], ("ctx", "sub"), split_axis=2, concat_axis=1, tiled=True)
    back = back.reshape(2, channels, tok_width)
    conv_rows, corr_rows = (back[0], back[1])
    partial_terms = jnp.sum(gated.astype(jnp.float32) * mixed.astype(jnp.float32), axis=1)
    grad_skip = lax.psum_scatter(partial_terms, ("ctx", "sub"), scatter_dimension=0, tiled=True)
    gain_col = skip_gain[:, None]
    forward_sum = conv_rows + gain_col * mixed.astype(jnp.float32)
    input_grad = corr_rows + gain_col * gated.astype(jnp.float32)
    output = (queries.astype(jnp.float32) * forward_sum).astype(jnp.bfloat16)
    grad_query = (out_grad.astype(jnp.float32) * forward_sum).astype(jnp.bfloat16)
    grad_key = (input_grad * value_branch.astype(jnp.float32)).astype(jnp.bfloat16)
    grad_value = (input_grad * key_branch.astype(jnp.float32)).astype(jnp.bfloat16)
    return (output, grad_query, grad_key, grad_value, grad_residue, grad_log_rate, grad_skip)


def solution(mesh):
    return jax.shard_map(
        body,
        mesh=mesh,
        in_specs=(
            P(None, ("ctx", "sub")),
            P(None, ("ctx", "sub")),
            P(None, ("ctx", "sub")),
            P(None, ("ctx", "sub")),
            P(("ctx", "sub"), None),
            P(("ctx", "sub"), None),
            P(),
        ),
        out_specs=(
            P(None, ("ctx", "sub")),
            P(None, ("ctx", "sub")),
            P(None, ("ctx", "sub")),
            P(None, ("ctx", "sub")),
            P(("ctx", "sub"), None),
            P(("ctx", "sub"), None),
            P(("ctx", "sub")),
        ),
        check_vma=False,
    )
```

profile of v0, /device:TPU:1, one launch (start us, length us, event | category | flops | bytes accessed | tf_op | source)
XLA Modules:
  0.0 271.3 jit_solution(15512212370317586998)
XLA Ops:
  2.9 12.0 %all-to-all-start = ((bf16[2,128,1,512]{3,0,2,1:T(2,128)(2,1)}), bf16[2,128,1,512]{3,0,2,1:T(2,128)(2,1)}, u32[]{:S(2)}, u32[]{:S(2)}) async-start(bf16[2,128,1,512]{3,0,2,1:T(2,128)(2,1)} %copy.109), calls=%async_computation | async-start | bytes 524288 | tf_op jit(solution)/shard_map/all_to_all | solution.py:160
  14.9 2.9 %broadcast_multiply_fusion = (f32[256,512]{0,1:T(8,128)}, f32[256,512]{0,1:T(8,128)S(1)}) fusion(), kind=kLoop, calls=%fused_computation.146 | loop fusion | flops 1966080 | bytes 1048576 | tf_op jit(solution)/shard_map/mul | solution.py:42
  17.9 39.4 %while.32 = (s32[]{:T(128)}, f32[1,65536]{1,0:T(1,128)S(1)}, f32[1,16]{1,0:T(1,128)S(1)}, f32[1,16]{1,0:T(1,128)S(1)}, s32[]{:T(128)}, /*index=5*/s32[]{:T(128)}) while((s32[]{:T(128)}, f32[1,65536]{1,0:T(1,128)S(1)}, f32[1,16]{1,0:T(1,128)S(1)}, f32[1,16]{1,0:T(1,128)S(1)}, s32[]{:T(128)}, /*index=5*/s32[]{:T(128)}) %tuple.98), condition=%wide.region_1.2_spmd.clone, body=%wide.region_0.1_spmd.clone.sunk | while | flops 327684 | bytes 1048691 | solution.py:125
  20.9 1.4 fusion.349
  23.4 1.4 fusion.349
  28.3 1.4 fusion.349
  30.8 1.4 fusion.349
  60.2 3.1 %multiply_subtract_fusion.2 = (f32[1,256,512]{1,2,0:T(8,128)S(1)}, f32[1,256,512]{1,2,0:T(8,128)S(1)}) fusion(f32[1,256,512]{1,2,0:T(8,128)S(1)} %convolution_bitcast_fusion.1, f32[128,512]{1,0:T(8,128)S(1)} %reshape.671), kind=kOutput, calls=%fused_computation.108 | convolution fusion | flops 204668928 | bytes 1835008 | tf_op jit(solution)/shard_map/ka,...ab->...kb/dot_general | solution.py:26
  69.0 1.6 fusion.76
  70.6 2.6 fusion.90
  73.3 67.5 %all-reduce = f32[128]{0:T(128)S(1)} all-reduce(f32[128]{0:T(128)S(1)} %get-tuple-element.296), channel_id=2, replica_groups=mesh['ctx'=32,'sub'=4] {'ctx','sub'}, use_global_device_ids=true, to_apply=%region_7.8.clone | all-reduce | flops 128 | bytes 1024
  144.5 3.6 %multiply_subtract_fusion.1 = (f32[2,1,256,512]{2,3,0,1:T(8,128)}, f32[2,1,256,512]{2,3,0,1:T(8,128)}) fusion(f32[2,1,256,512]{2,3,0,1:T(8,128)S(1)} %convolution_bitcast_fusion, f32[256,512]{0,1:T(8,128)} %get-tuple-element.325, f32[256,512]{0,1:T(8,128)S(1)} %get-tuple-element.326, bf16[2,128,1,512]{1,3,0,2:T(8,128)(2,1)S(1)} %copy.110), kind=kOutput, calls=%fused_computation.64 | convolution fusion | flops 404946944 | bytes 4456448 | tf_op jit(solution)/shard_map/ka,...ab->...kb/dot_general | solution.py:26
  148.0 1.6 copy.112
  149.6 2.9 %fusion.172 = f32[2,256,128,4]{2,3,1,0:T(4,128)} fusion(f32[2,256,4,128]{3,2,1,0:T(4,128)S(1)} %copy.112), kind=kOutput, calls=%fused_computation.226 | convolution fusion | flops 12583136 | bytes 2097152 | tf_op jit(solution)/shard_map/pq,...qb->...pb/dot_general | solution.py:54
  152.5 1.6 copy.111
  154.2 1.9 fusion.174
  156.1 2.1 fusion.26
  158.2 2.6 subtract_bitcast_fusion.1
  167.9 1.7 fusion.41
  169.6 1.7 fusion.40
  171.3 1.7 convolution_subtract_fusion
  173.0 2.2 multiply_subtract_fusion
  175.2 3.7 %fusion.19 = f32[3,256,128,4]{2,3,1,0:T(4,128)S(1)} fusion(f32[3,256,4,128]{3,1,2,0:T(8,128)S(1)} %get-tuple-element.302), kind=kOutput, calls=%fused_computation.32 | convolution fusion | flops 18874592 | bytes 3145728 | tf_op jit(solution)/shard_map/pq,...qb->...pb/dot_general | solution.py:54
  178.9 5.7 %fusion.23 = f32[3,256,128,4]{2,3,1,0:T(4,128)} fusion(f32[3,256,4,128]{3,1,2,0:T(8,128)S(1)} %get-tuple-element.301), kind=kOutput, calls=%fused_computation.36 | convolution fusion | flops 18874592 | bytes 3145728 | tf_op jit(solution)/shard_map/pq,...qb->...pb/dot_general | solution.py:54
  184.6 5.9 %add_bitcast_fusion = f32[3,1,256,4,128]{4,3,2,0,1:T(4,128)} fusion(f32[3,256,128,4]{2,3,1,0:T(4,128)S(1)} %fusion.19, f32[3,256,4,128]{3,1,2,0:T(8,128)S(1)} %get-tuple-element.301), kind=kOutput, calls=%fused_computation.25 | convolution fusion | flops 19267808 | bytes 4718592 | tf_op jit(solution)/shard_map/pq,...qb->...pb/dot_general | solution.py:54
  190.4 1.7 copy.146
  192.1 7.2 %subtract_bitcast_fusion = f32[3,1,256,4,128]{4,3,2,0,1:T(4,128)} fusion(f32[3,256,128,4]{2,3,1,0:T(4,128)} %fusion.23, f32[3,256,4,128]{3,1,2,0:T(8,128)S(1)} %get-tuple-element.302), kind=kOutput, calls=%fused_computation.27 | convolution fusion | flops 19267808 | bytes 4718592 | tf_op jit(solution)/shard_map/pq,...qb->...pb/dot_general | solution.py:54
  199.3 1.7 copy.145
  201.0 3.2 %fusion.11 = f32[3,512,128]{2,1,0:T(8,128)S(1)} fusion(f32[3,256,512]{1,2,0:T(8,128)S(1)} %bitcast.274, f32[3,256,512]{1,2,0:T(8,128)S(1)} %bitcast.276, f32[256,512]{0,1:T(8,128)} %fusion.90, f32[256,512]{0,1:T(8,128)} %copy-done), kind=kOutput, calls=%fused_computation.18 | convolution fusion | flops 605618176 | bytes 4980736 | tf_op jit(solution)/shard_map/ak,...kb->...ab/dot_general | solution.py:35
  204.3 2.0 fusion.34
  208.2 4.7 %all-to-all-start.1 = ((f32[2,1,128,512]{3,1,0,2:T(1,128)}), f32[2,1,128,512]{3,1,0,2:T(1,128)S(1)}, u32[]{:S(2)}, u32[]{:S(2)}) async-start(f32[2,1,128,512]{3,1,0,2:T(1,128)} %copy.135), calls=%async_computation.1 | async-start | bytes 1048576 | tf_op jit(solution)/shard_map/all_to_all | solution.py:187
  213.2 55.5 %while.31 = (s32[]{:T(128)}, f32[1,16]{1,0:T(1,128)S(1)}, f32[1,16]{1,0:T(1,128)S(1)}, f32[1,65536]{1,0:T(1,128)S(1)}, f32[1,16]{1,0:T(1,128)S(1)}, /*index=5*/s32[]{:T(128)}, s32[]{:T(128)}) while((s32[]{:T(128)}, f32[1,16]{1,0:T(1,128)S(1)}, f32[1,16]{1,0:T(1,128)S(1)}, f32[1,65536]{1,0:T(1,128)S(1)}, ...), condition=%wide.region_5.6_spmd.clone.clone, body=%wide.region_2.5_spmd.clone.clone.sunk | while | flops 393217 | bytes 262277 | solution.py:146
  213.8 1.4 fusion.348
  217.1 1.4 fusion.348
  220.6 1.4 fusion.348
  224.1 1.4 fusion.348
  227.5 1.4 fusion.348
  231.0 1.4 fusion.348
  234.5 1.4 fusion.348
  237.9 1.4 fusion.348
  241.4 1.4 fusion.348
  244.9 1.4 fusion.348
  248.4 1.4 fusion.348
  251.8 1.4 fusion.348
  255.3 1.4 fusion.348
  258.8 1.4 fusion.348
  262.3 1.4 fusion.348
  265.7 1.4 fusion.348
  (158 shorter events, 92.9 us)
Async XLA Ops:
  0.6 17.2 %copy-start.11 = (f32[1,16]{1,0:T(1,128)S(1)}, f32[1,16]{1,0:T(1,128)}, u32[]{:S(2)}) copy-start(f32[1,16]{1,0:T(1,128)} %param.16) | copy-start | bytes 196
  0.6 17.2 %copy-start.10 = (f32[1,16]{1,0:T(1,128)S(1)}, f32[1,16]{1,0:T(1,128)}, u32[]{:S(2)}) copy-start(f32[1,16]{1,0:T(1,128)} %param.15) | copy-start | bytes 196
  2.9 139.3 %all-to-all-start = ((bf16[2,128,1,512]{3,0,2,1:T(2,128)(2,1)}), bf16[2,128,1,512]{3,0,2,1:T(2,128)(2,1)}, u32[]{:S(2)}, u32[]{:S(2)}) async-start(bf16[2,128,1,512]{3,0,2,1:T(2,128)(2,1)} %copy.109), calls=%async_computation | async-start | bytes 524288 | tf_op jit(solution)/shard_map/all_to_all | solution.py:160
  17.8 126.7 %copy-start = (f32[256,512]{0,1:T(8,128)}, f32[256,512]{0,1:T(8,128)S(1)}, u32[]{:S(2)}) copy-start(f32[256,512]{0,1:T(8,128)S(1)} %get-tuple-element.326) | copy-start | bytes 1572868
  154.2 1.9 copy-start.3
  165.8 1.0 copy-start.5
  201.0 3.2 %copy-start.1 = (f32[256,512]{0,1:T(8,128)S(1)}, f32[256,512]{0,1:T(8,128)}, u32[]{:S(2)}) copy-start(f32[256,512]{0,1:T(8,128)} %copy-done) | copy-start | bytes 1572868
  201.0 3.2 %copy-start.2 = (f32[256,512]{0,1:T(8,128)S(1)}, f32[256,512]{0,1:T(8,128)}, u32[]{:S(2)}) copy-start(f32[256,512]{0,1:T(8,128)} %fusion.90) | copy-start | bytes 1572868
  206.3 0.9 copy-start.4
  207.2 5.8 %slice-start = ((f32[3,1,128,512]{2,3,0,1:T(8,128)}), f32[1,1,128,512]{2,3,0,1:T(8,128)S(1)}, s32[]{:S(2)}) async-start(f32[3,1,128,512]{2,3,0,1:T(8,128)} %copy-done.4), calls=%async_computation.2 | async-start | bytes 524288 | tf_op jit(solution)/shard_map/slice | solution.py:185
  208.2 61.4 %all-to-all-start.1 = ((f32[2,1,128,512]{3,1,0,2:T(1,128)}), f32[2,1,128,512]{3,1,0,2:T(1,128)S(1)}, u32[]{:S(2)}, u32[]{:S(2)}) async-start(f32[2,1,128,512]{3,1,0,2:T(1,128)} %copy.135), calls=%async_computation.1 | async-start | bytes 1048576 | tf_op jit(solution)/shard_map/all_to_all | solution.py:187
  212.9 57.1 %copy-start.6 = (bf16[128,512]{1,0:T(8,128)(2,1)S(1)}, bf16[128,512]{1,0:T(8,128)(2,1)}, u32[]{:S(2)}) copy-start(bf16[128,512]{1,0:T(8,128)(2,1)} %param.12) | copy-start | bytes 393220
  212.9 57.1 %copy-start.7 = (bf16[128,512]{1,0:T(8,128)(2,1)S(1)}, bf16[128,512]{1,0:T(8,128)(2,1)}, u32[]{:S(2)}) copy-start(bf16[128,512]{1,0:T(8,128)(2,1)} %param.11) | copy-start | bytes 393220
  213.0 57.1 %copy-start.8 = (bf16[128,512]{1,0:T(8,128)(2,1)S(1)}, bf16[128,512]{1,0:T(8,128)(2,1)}, u32[]{:S(2)}) copy-start(bf16[128,512]{1,0:T(8,128)(2,1)} %param.14) | copy-start | bytes 393220
  213.0 57.1 %copy-start.9 = (bf16[128,512]{1,0:T(8,128)(2,1)S(1)}, bf16[128,512]{1,0:T(8,128)(2,1)}, u32[]{:S(2)}) copy-start(bf16[128,512]{1,0:T(8,128)(2,1)} %param.13) | copy-start | bytes 393220
  213.0 57.1 %copy-start.12 = (f32[128]{0:T(128)S(1)}, f32[128]{0:T(128)}, u32[]{:S(2)}) copy-start(f32[128]{0:T(128)} %param.17) | copy-start | bytes 1540
where the time goes:
time: 275 us; the launch traced here: 271 us
  other arithmetic  80.5 us (29%)
  blocking collectives  67.5 us (25%)
  matrix products  66.8 us (24%)
  local copies, waits for them, and re-layouts  37.8 us (14%)
  starting transfers between devices  16.6 us (6%)
    unnamed x1, blocking collectives  67.5 us
    dot_general x12, matrix products, contract(): jnp.einsum('pq,...qb->...pb', matrix, values, precision=FULL_PRECISION)  36.4 us
    reduce_sum x16, other arithmetic, one_mode(): jnp.sum(weighted * positions[None, :], axis=1, keepdims=True)  21.9 us
    mul x16, other arithmetic, add_mode(): return total + weight * jnp.exp(-speed * positions[None, :])  21.6 us
    dot_general x12, matrix products, contract(): jnp.einsum('...bq,qp->...bp', values, matrix, precision=FULL_PRECISION)  16.5 us
    dynamic_update_slice x16, local copies, waits for them, and re-layouts, one_mode(): lax.dynamic_update_slice_in_dim(timed_sums, jnp.sum(weighted * positions[...  12.1 us
    dynamic_update_slice x16, local copies, waits for them, and re-layouts, one_mode(): lax.dynamic_update_slice_in_dim(plain_sums, jnp.sum(weighted, axis=1, kee...  12 us
    all_to_all x1, starting transfers between devices, body(): lax.all_to_all(paired[:, :, None, :], ('ctx', 'sub'), split_axis=1, conca...  12 us
  transfers between devices with their start and end apart: 2, of which 0 were waited for; matrix products, arithmetic and copies ran while one was open for 43% of the time, Pallas kernels for 0%

commit v1 on v0

v1 whole, which is shorter than its diff:
```python
import functools

import jax
import jax.numpy as jnp
from jax import lax
from jax.experimental import pallas as pl
from jax.experimental.pallas import tpu as pltpu
from jax.sharding import PartitionSpec as P

MESH = pl.DeviceIdType.MESH
FULL = lax.Precision.HIGHEST
NT = (((1,), (1,)), ((), ()))
TN = (((0,), (0,)), ((), ()))
LANES = 128


def iota(shape, axis):
    return lax.broadcasted_iota(jnp.int32, shape, axis)


def column(row):
    n = row.shape[1]
    eye = iota((n, n), 0) == iota((n, n), 1)
    return jnp.sum(jnp.where(eye, row, 0.0), axis=1, keepdims=True)


def shifted(rows, count):
    n = rows.shape[0]
    if count > 0:
        moved = pltpu.roll(rows, count, 0)
        return jnp.where(iota(rows.shape, 0) >= count, moved, 0.0)
    moved = pltpu.roll(rows, n + count, 0)
    return jnp.where(iota(rows.shape, 0) < n + count, moved, 0.0)


def running(rows, speed, span, sign):
    n = rows.shape[0]
    step = 1
    while step < n:
        rows = rows + jnp.exp(-speed * float(span * step)) * shifted(rows, sign * step)
        step *= 2
    return shifted(rows, sign)


def send_all(devices, sub, me, src, dst, send_sem, recv_sem):
    def one(k, carry):
        peer = lax.rem(me + k, devices)
        pltpu.make_async_remote_copy(
            src_ref=src.at[peer],
            dst_ref=dst.at[me],
            send_sem=send_sem,
            recv_sem=recv_sem,
            device_id=(peer // sub, lax.rem(peer, sub)),
            device_id_type=MESH,
        ).start()
        return carry

    lax.fori_loop(1, devices, one, 0)


def whole(devices, sub, me, src, dst, send_sem, recv_sem):
    peer = lax.rem(me + 1, devices)
    return pltpu.make_async_remote_copy(
        src_ref=src.at[pl.ds(0, devices - 1)],
        dst_ref=dst.at[pl.ds(0, devices - 1)],
        send_sem=send_sem,
        recv_sem=recv_sem,
        device_id=(peer // sub, lax.rem(peer, sub)),
        device_id_type=MESH,
    )


def exchange_kernel(
    devices, sub, q_ref, k_ref, v_ref, og_ref, res_ref, rate_ref,
    conv_ref, corr_ref, row_ref,
    stage, toep, out_buf, in_buf, back_buf, home_buf,
    out_send, out_recv, back_send, back_recv,
):
    me = lax.axis_index("ctx") * sub + lax.axis_index("sub")
    channels, width = q_ref.shape
    blocks = width // LANES
    slab = 2 * blocks
    modes = res_ref.shape[1]
    barrier = pltpu.get_barrier_semaphore()

    def greet(k, carry):
        peer = lax.rem(me + k, devices)
        pl.semaphore_signal(
            barrier, inc=1, device_id=(peer // sub, lax.rem(peer, sub)), device_id_type=MESH
        )
        return carry

    lax.fori_loop(1, devices, greet, 0)

    f32, bf16 = jnp.float32, jnp.bfloat16

    def spread(first, second):
        for j in range(blocks):
            cols = slice(j * LANES, (j + 1) * LANES)
            stage[pl.ds(j, channels, stride=slab), :] = first(cols)
            stage[pl.ds(blocks + j, channels, stride=slab), :] = second(cols)
        return stage[...].astype(bf16).reshape(channels, slab, LANES)

    out_buf[...] = spread(
        lambda c: k_ref[:, c].astype(f32) * v_ref[:, c].astype(f32),
        lambda c: og_ref[:, c].astype(f32) * q_ref[:, c].astype(f32),
    )
    pl.semaphore_wait(barrier, devices - 1)
    send_all(devices, sub, me, out_buf, in_buf, out_send, out_recv)
    in_buf[me] = out_buf[me]

    speed_row = jnp.exp(rate_ref[...])
    res_row = res_ref[...]
    speed = column(speed_row)
    res = column(res_row)
    pos = iota((modes, width), 1).astype(f32)
    rise = jnp.exp(-speed * pos)
    fall = jnp.exp(-speed * (width - 1.0 - pos))
    to_end = fall.astype(bf16)
    to_end_timed = (fall * (width - 1.0 - pos)).astype(bf16)
    to_start = rise.astype(bf16)
    to_start_timed = (rise * pos).astype(bf16)
    from_before = (res * jnp.exp(-speed * (pos + 1.0))).astype(bf16)
    from_after = (res * jnp.exp(-speed * (width - pos))).astype(bf16)
    grow = jnp.exp(speed * iota((modes, LANES), 1).astype(f32))
    lag = iota((LANES, width), 1) - iota((LANES, width), 0)
    near = lax.dot_general(grow, res * rise, TN, precision=FULL, preferred_element_type=f32)
    near = jnp.where(lag >= 0, near, 0.0).astype(bf16)
    for row in range(blocks):
        rows = slice(row * LANES, (row + 1) * LANES)
        if row:
            toep[rows, : row * LANES] = jnp.zeros((LANES, row * LANES), bf16)
        toep[rows, row * LANES :] = near[:, : width - row * LANES]

    whole(devices, sub, me, out_buf, in_buf, out_send, out_recv).wait_recv()
    stage[...] = in_buf[...].reshape(devices * slab, LANES).astype(f32)

    def gathered(start):
        parts = [stage[pl.ds(start + j, devices, stride=slab), :] for j in range(blocks)]
        return jnp.concatenate(parts, axis=1).astype(bf16)

    mixed, gated = gathered(0), gathered(blocks)

    def state(rows, weights):
        return lax.dot_general(rows, weights, NT, preferred_element_type=f32)

    ends, starts = state(mixed, to_end), state(gated, to_start)
    before = running(ends, speed_row, width, 1)
    after = running(starts, speed_row, width, -1)
    conv = jnp.dot(mixed, toep[...], preferred_element_type=f32)
    conv = conv + jnp.dot(before.astype(bf16), from_before, preferred_element_type=f32)
    corr = lax.dot_general(gated, toep[...], NT, preferred_element_type=f32)
    corr = corr + jnp.dot(after.astype(bf16), from_after, preferred_element_type=f32)
    back_buf[...] = spread(lambda c: conv[:, c], lambda c: corr[:, c])
    send_all(devices, sub, me, back_buf, home_buf, back_send, back_recv)
    home_buf[me] = back_buf[me]

    pairs = lax.dot_general(mixed, gated, TN, preferred_element_type=f32)
    lagged = []
    for k in range(blocks):
        total = pairs[:LANES, k * LANES : (k + 1) * LANES]
        for row in range(1, blocks - k):
            rows = slice(row * LANES, (row + 1) * LANES)
            total = total + pairs[rows, (row + k) * LANES : (row + k + 1) * LANES]
        lagged.append(total)
    lagged = jnp.where(lag >= 0, jnp.concatenate(lagged, axis=1), 0.0)
    skip_sum = jnp.sum(jnp.where(lag == 0, lagged, 0.0), keepdims=True)

    def local_sum(values):
        by_lag = jnp.dot(grow, values, precision=FULL, preferred_element_type=f32)
        return jnp.sum(by_lag * rise, axis=1, keepdims=True)

    plain_col = local_sum(lagged)
    timed_col = local_sum(lagged * lag.astype(f32))
    eye = iota((modes, modes), 0) == iota((modes, modes), 1)

    def as_row(col):
        return jnp.sum(jnp.where(eye, col, 0.0), axis=0, keepdims=True)

    one_step = jnp.exp(-speed_row)
    chunk_step = jnp.exp(-speed_row * float(width))
    ends_timed, starts_timed = state(mixed, to_end_timed), state(gated, to_start_timed)
    cross = before * starts
    cross_timed = ends_timed * after + before * starts_timed + cross
    cross_timed = cross_timed + (float(width) * chunk_step) * (before * after)
    plain = as_row(plain_col) + one_step * jnp.sum(cross, axis=0, keepdims=True)
    timed = as_row(timed_col) + one_step * jnp.sum(cross_timed, axis=0, keepdims=True)
    seq_len = devices * width
    row_ref[0:1, :] = jnp.zeros((1, LANES), f32)
    row_ref[0:1, 0:modes] = plain * (1.0 / seq_len)
    row_ref[0:1, modes : 2 * modes] = -res_row * speed_row * timed * (1.0 / seq_len**0.5)
    row_ref[0:1, 2 * modes : 2 * modes + 1] = skip_sum

    whole(devices, sub, me, back_buf, home_buf, back_send, back_recv).wait_recv()
    stage[...] = home_buf[...].reshape(channels * slab, LANES).astype(f32)
    for j in range(blocks):
        cols = slice(j * LANES, (j + 1) * LANES)
        conv_ref[:, cols] = stage[pl.ds(j, channels, stride=slab), :].astype(bf16)
        corr_ref[:, cols] = stage[pl.ds(blocks + j, channels, stride=slab), :].astype(bf16)
    whole(devices, sub, me, out_buf, in_buf, out_send, out_recv).wait_send()
    whole(devices, sub, me, back_buf, home_buf, back_send, back_recv).wait_send()


def finish_kernel(
    q_ref, k_ref, v_ref, og_ref, gain_ref, conv_ref, corr_ref, row_ref,
    out_ref, gq_ref, gk_ref, gv_ref, gres_ref, grate_ref, gskip_ref,
):
    f32, bf16 = jnp.float32, jnp.bfloat16
    modes = gres_ref.shape[1]
    gain = column(gain_ref[...])
    q, k = q_ref[...].astype(f32), k_ref[...].astype(f32)
    v, og = v_ref[...].astype(f32), og_ref[...].astype(f32)
    mixed = (k * v).astype(bf16).astype(f32)
    gated = (og * q).astype(bf16).astype(f32)
    forward_sum = conv_ref[...].astype(f32) + gain * mixed
    input_grad = corr_ref[...].astype(f32) + gain * gated
    out_ref[...] = (q * forward_sum).astype(bf16)
    gq_ref[...] = (og * forward_sum).astype(bf16)
    gk_ref[...] = (input_grad * v).astype(bf16)
    gv_ref[...] = (input_grad * k).astype(bf16)
    gres_ref[...] = row_ref[:, 0:modes]
    grate_ref[...] = row_ref[:, modes : 2 * modes]
    gskip_ref[...] = row_ref[:, 2 * modes : 2 * modes + 1]


def body(queries, key_branch, value_branch, out_grad, residue, log_rate, skip_gain):
    sub = lax.axis_size("sub")
    devices = lax.axis_size("ctx") * sub
    channels, width = queries.shape
    modes = residue.shape[1]
    slab = 2 * width // LANES
    f32, bf16 = jnp.float32, jnp.bfloat16
    vmem = pl.BlockSpec(memory_space=pltpu.VMEM)
    wide = jax.ShapeDtypeStruct((channels, width), bf16)
    conv, corr, row = pl.pallas_call(
        functools.partial(exchange_kernel, devices, sub),
        out_shape=(wide, wide, jax.ShapeDtypeStruct((1, LANES), f32)),
        in_specs=[vmem] * 6,
        out_specs=(vmem,) * 3,
        scratch_shapes=[
            pltpu.VMEM((channels * slab, LANES), f32),
            pltpu.VMEM((width, width), bf16),
            pltpu.VMEM((channels, slab, LANES), bf16),
            pltpu.VMEM((devices, slab, LANES), bf16),
            pltpu.VMEM((devices, slab, LANES), bf16),
            pltpu.VMEM((channels, slab, LANES), bf16),
            pltpu.SemaphoreType.DMA,
            pltpu.SemaphoreType.DMA,
            pltpu.SemaphoreType.DMA,
            pltpu.SemaphoreType.DMA,
        ],
        compiler_params=pltpu.CompilerParams(
            collective_id=0, has_side_effects=True, vmem_limit_bytes=32 * 2**20
        ),
        name="exchange",
    )(queries, key_branch, value_branch, out_grad, residue, log_rate)
    output, grad_query, grad_key, grad_value, grad_residue, grad_rate, grad_skip = pl.pallas_call(
        finish_kernel,
        out_shape=(wide,) * 4
        + (jax.ShapeDtypeStruct((1, modes), f32),) * 2
        + (jax.ShapeDtypeStruct((1, 1), f32),),
        in_specs=[vmem] * 8,
        out_specs=(vmem,) * 7,
        compiler_params=pltpu.CompilerParams(vmem_limit_bytes=32 * 2**20),
        name="finish",
    )(queries, key_branch, value_branch, out_grad, skip_gain[None, :], conv, corr, row)
    return (
        output, grad_query, grad_key, grad_value, grad_residue, grad_rate, grad_skip.reshape(1)
    )


def solution(mesh):
    wide = P(None, ("ctx", "sub"))
    rows = P(("ctx", "sub"), None)
    return jax.shard_map(
        body,
        mesh=mesh,
        in_specs=(wide, wide, wide, wide, rows, rows, P()),
        out_specs=(wide, wide, wide, wide, rows, rows, P(("ctx", "sub"))),
        check_vma=False,
    )
```

time: 275 us -> 34.9 us (0.13); the launches traced: 271 us -> 34.7 us
  other arithmetic: 80.5 us -> 0 us
  blocking collectives: 67.5 us -> 0 us
  matrix products: 66.8 us -> 0 us
  local copies, waits for them, and re-layouts: 37.8 us -> 4.92 us
  Pallas kernels: 0 us -> 29.1 us
  starting transfers between devices: 16.6 us -> 0 us
    unnamed x1 -> x0, blocking collectives: 67.5 us -> none
    dot_general x30 -> x0, matrix products: 66.8 us -> none  [the longest x12 36.4 us: contract(): jnp.einsum('pq,...qb->...pb', matrix, values, precision=FULL_PRECISION)]
    pallas_call x0 -> x2, Pallas kernels: none -> 29.1 us  [the longest x1 28.1 us: body(): pl.pallas_call(functools.partial(exchange_kernel, devices, sub), out_shap...]
    mul x17 -> x0, other arithmetic: 24.5 us -> none  [the longest x16 21.6 us: add_mode(): return total + weight * jnp.exp(-speed * positions[None, :])]
    dynamic_update_slice x32 -> x0, local copies, waits for them, and re-layouts: 24 us -> none  [the longest x16 12.1 us: one_mode(): lax.dynamic_update_slice_in_dim(timed_sums, jnp.sum(weighted * positions[...]
    reduce_sum x17 -> x0, other arithmetic: 23.2 us -> none  [the longest x16 21.9 us: one_mode(): jnp.sum(weighted * positions[None, :], axis=1, keepdims=True)]
    all_to_all x2 -> x0, starting transfers between devices: 16.6 us -> none  [the longest x1 12 us: body(): lax.all_to_all(paired[:, :, None, :], ('ctx', 'sub'), split_axis=1, conca...]
    dynamic_slice x16 -> x0, other arithmetic: 9.47 us -> none  [add_mode(): weight = lax.dynamic_slice_in_dim(residue, mode_idx, 1, 1)]
  transfers between devices with their start and end apart: 2 -> 0, of which waited for: 0 -> 0; matrix products, arithmetic and copies ran while one was open for 43% -> 0% of each run, Pallas kernels for 0% -> 0%
where the time goes in v1:
time: 34.9 us; the launch traced here: 34.7 us
  Pallas kernels  29.1 us (83%)
  local copies, waits for them, and re-layouts  4.92 us (14%)
  between operations  0.67 us (2%)
    pallas_call x1, Pallas kernels, body(): pl.pallas_call(functools.partial(exchange_kernel, devices, sub), out_shap...  28.1 us
    unnamed x14, local copies, waits for them, and re-layouts  4.92 us
    pallas_call x1, Pallas kernels, body(): pl.pallas_call(finish_kernel, out_shape=(wide,) * 4 + (jax.ShapeDtypeStru...  1.03 us

profile of v1, /device:TPU:1, one launch (start us, length us, event | category | flops | bytes accessed | tf_op | source)
XLA Modules:
  0.0 34.7 jit_solution(5059321645871219210)
XLA Ops:
  0.6 0.0 copy-start.6
  0.6 0.0 copy-start.5
  0.7 0.6 %copy-done.6 = f32[1,16]{1,0:T(1,128)S(1)} copy-done((f32[1,16]{1,0:T(1,128)S(1)}, f32[1,16]{1,0:T(1,128)}, u32[]{:S(2)}) %copy-start.6) | copy-done | bytes 88
  1.3 0.0 copy-done.5
  1.3 0.0 copy-start
  1.3 0.9 %copy-done = bf16[128,512]{1,0:T(8,128)(2,1)S(1)} copy-done((bf16[128,512]{1,0:T(8,128)(2,1)S(1)}, bf16[128,512]{1,0:T(8,128)(2,1)}, u32[]{:S(2)}) %copy-start) | copy-done | bytes 131096
  2.2 0.0 copy-start.1
  2.2 0.9 %copy-done.1 = bf16[128,512]{1,0:T(8,128)(2,1)S(1)} copy-done((bf16[128,512]{1,0:T(8,128)(2,1)S(1)}, bf16[128,512]{1,0:T(8,128)(2,1)}, u32[]{:S(2)}) %copy-start.1) | copy-done | bytes 131096
  3.1 0.0 copy-start.2
  3.1 0.9 %copy-done.2 = bf16[128,512]{1,0:T(8,128)(2,1)S(1)} copy-done((bf16[128,512]{1,0:T(8,128)(2,1)S(1)}, bf16[128,512]{1,0:T(8,128)(2,1)}, u32[]{:S(2)}) %copy-start.2) | copy-done | bytes 131096
  4.0 0.0 copy-start.3
  4.0 0.9 %copy-done.3 = bf16[128,512]{1,0:T(8,128)(2,1)S(1)} copy-done((bf16[128,512]{1,0:T(8,128)(2,1)S(1)}, bf16[128,512]{1,0:T(8,128)(2,1)}, u32[]{:S(2)}) %copy-start.3) | copy-done | bytes 131096
  4.9 28.1 %exchange.1 = (bf16[128,512]{1,0:T(8,128)(2,1)S(1)}, bf16[128,512]{1,0:T(8,128)(2,1)S(1)}, f32[1,128]{1,0:T(1,128)S(1)}) custom-call(bf16[128,512]{1,0:T(8,128)(2,1)S(1)} %copy-done, bf16[128,512]{1,0:T(8,128)(2,1)S(1)} %copy-done.1, bf16[128,512]{1,0:T(8,128)(2,1)S(1)} %copy-done.2, bf16[128,512]{1,0:T(8,128)(2,1)S(1)} %copy-done.3, f32[1,16]{1,0:T(1,128)S(1)} %copy-done.5, ...), custom_call_target="tpu_custom_call" | custom-call | tf_op jit(solution)/shard_map/exchange/pallas_call | solution.py:235
  33.0 0.0 copy-start.4
  33.1 0.6 %copy-done.4 = f32[128]{0:T(128)S(1)} copy-done((f32[128]{0:T(128)S(1)}, f32[128]{0:T(128)}, u32[]{:S(2)}) %copy-start.4) | copy-done | bytes 536
  33.7 1.0 %finish.1 = (bf16[128,512]{1,0:T(8,128)(2,1)}, bf16[128,512]{1,0:T(8,128)(2,1)}, bf16[128,512]{1,0:T(8,128)(2,1)}, bf16[128,512]{1,0:T(8,128)(2,1)}, f32[1,16]{1...) custom-call(bf16[128,512]{1,0:T(8,128)(2,1)S(1)} %copy-done, bf16[128,512]{1,0:T(8,128)(2,1)S(1)} %copy-done.1, ...), custom_call_target="tpu_custom_call" | custom-call | tf_op jit(solution)/shard_map/finish/pallas_call | solution.py:257
Async XLA Ops:
  0.6 0.7 %copy-start.6 = (f32[1,16]{1,0:T(1,128)S(1)}, f32[1,16]{1,0:T(1,128)}, u32[]{:S(2)}) copy-start(f32[1,16]{1,0:T(1,128)} %rate_ref.1) | copy-start | bytes 196
  0.6 0.7 %copy-start.5 = (f32[1,16]{1,0:T(1,128)S(1)}, f32[1,16]{1,0:T(1,128)}, u32[]{:S(2)}) copy-start(f32[1,16]{1,0:T(1,128)} %res_ref.1) | copy-start | bytes 196
  1.3 0.9 %copy-start = (bf16[128,512]{1,0:T(8,128)(2,1)S(1)}, bf16[128,512]{1,0:T(8,128)(2,1)}, u32[]{:S(2)}) copy-start(bf16[128,512]{1,0:T(8,128)(2,1)} %q_ref.3) | copy-start | bytes 393220
  2.2 0.9 %copy-start.1 = (bf16[128,512]{1,0:T(8,128)(2,1)S(1)}, bf16[128,512]{1,0:T(8,128)(2,1)}, u32[]{:S(2)}) copy-start(bf16[128,512]{1,0:T(8,128)(2,1)} %k_ref.3) | copy-start | bytes 393220
  3.1 0.9 %copy-start.2 = (bf16[128,512]{1,0:T(8,128)(2,1)S(1)}, bf16[128,512]{1,0:T(8,128)(2,1)}, u32[]{:S(2)}) copy-start(bf16[128,512]{1,0:T(8,128)(2,1)} %v_ref.3) | copy-start | bytes 393220
  4.0 0.9 %copy-start.3 = (bf16[128,512]{1,0:T(8,128)(2,1)S(1)}, bf16[128,512]{1,0:T(8,128)(2,1)}, u32[]{:S(2)}) copy-start(bf16[128,512]{1,0:T(8,128)(2,1)} %og_ref.3) | copy-start | bytes 393220
  33.0 0.7 %copy-start.4 = (f32[128]{0:T(128)S(1)}, f32[128]{0:T(128)}, u32[]{:S(2)}) copy-start(f32[128]{0:T(128)} %param.13) | copy-start | bytes 1540

commit v2 on v1

--- a/solution.py
+++ b/solution.py
@@ -42,55 +42,76 @@
     return shifted(rows, sign)
 
 
-def send_all(devices, sub, me, src, dst, send_sem, recv_sem):
-    def one(k, carry):
-        peer = lax.rem(me + k, devices)
+def partners(me):
+    core, z = me % 2, me // 4 % 4
+    y, x = me // 2 % 2 * 2 + me // 16 % 2, me // 32
+    across = [lax.rem(x + d, 4) * 8 for d in range(4)]
+    along = [lax.rem(z + d, 4) for d in range(4)]
+    ups = [lax.rem(y + d, 4) for d in range(4)]
+    high = [[u // 2 * 2 + lax.rem(core + d, 2) for d in range(2)] for u in ups]
+    low = [lax.rem(u, 2) * 4 for u in ups]
+    moves = [
+        (dx, dy, dz, dc)
+        for dx in range(4) for dy in range(4) for dz in range(4) for dc in range(2)
+        if (dx, dy, dz, dc) != (0, 0, 0, 0)
+    ]
+    moves.sort(key=lambda m: -sum(min(d, 4 - d) for d in m[:3]))
+    found = []
+    for dx, dy, dz, dc in moves:
+        ctx, sub = across[dx] + low[dy] + along[dz], high[dy][dc]
+        found.append((ctx * 4 + sub, (ctx, sub)))
+    return found
+
+
+def send_all(peers, me, src, dst, send_sem, recv_sem):
+    for peer, place in peers:
         pltpu.make_async_remote_copy(
             src_ref=src.at[peer],
             dst_ref=dst.at[me],
             send_sem=send_sem,
             recv_sem=recv_sem,
-            device_id=(peer // sub, lax.rem(peer, sub)),
+            device_id=place,
             device_id_type=MESH,
         ).start()
-        return carry
-
-    lax.fori_loop(1, devices, one, 0)
-
-
-def whole(devices, sub, me, src, dst, send_sem, recv_sem):
-    peer = lax.rem(me + 1, devices)
+
+
+def whole(peers, src, dst, send_sem, recv_sem):
     return pltpu.make_async_remote_copy(
-        src_ref=src.at[pl.ds(0, devices - 1)],
-        dst_ref=dst.at[pl.ds(0, devices - 1)],
+        src_ref=src.at[pl.ds(0, len(peers))],
+        dst_ref=dst.at[pl.ds(0, len(peers))],
         send_sem=send_sem,
         recv_sem=recv_sem,
-        device_id=(peer // sub, lax.rem(peer, sub)),
+        device_id=peers[0][1],
         device_id_type=MESH,
     )
 
 
 def exchange_kernel(
-    devices, sub, q_ref, k_ref, v_ref, og_ref, res_ref, rate_ref,
-    conv_ref, corr_ref, row_ref,
-    stage, toep, out_buf, in_buf, back_buf, home_buf,
-    out_send, out_recv, back_send, back_recv,
+    devices, sub, q_hbm, k_hbm, v_hbm, og_hbm, res_hbm, rate_hbm, gain_hbm,
+    conv_ref, corr_ref, row_ref, q_ref, k_ref, v_ref, og_ref, gain_ref,
+    res_ref, rate_ref, stage, toep, out_buf, in_buf, back_buf, home_buf,
+    load_sems, out_send, out_recv, back_send, back_recv,
 ):
     me = lax.axis_index("ctx") * sub + lax.axis_index("sub")
     channels, width = q_ref.shape
     blocks = width // LANES
     slab = 2 * blocks
     modes = res_ref.shape[1]
+    peers = partners(me)
     barrier = pltpu.get_barrier_semaphore()
-
-    def greet(k, carry):
-        peer = lax.rem(me + k, devices)
-        pl.semaphore_signal(
-            barrier, inc=1, device_id=(peer // sub, lax.rem(peer, sub)), device_id_type=MESH
+    for _, place in peers:
+        pl.semaphore_signal(barrier, inc=1, device_id=place, device_id_type=MESH)
+    loads = [
+        pltpu.make_async_copy(src, dst, load_sems.at[i])
+        for i, (src, dst) in enumerate(
+            [(k_hbm, k_ref), (v_hbm, v_ref), (og_hbm, og_ref), (q_hbm, q_ref),
+             (res_hbm, res_ref), (rate_hbm, rate_ref), (gain_hbm, gain_ref)]
         )
-        return carry
-
-    lax.fori_loop(1, devices, greet, 0)
+    ]
+    for load in loads:
+        load.start()
+    for load in loads:
+        load.wait()
 
     f32, bf16 = jnp.float32, jnp.bfloat16
 
@@ -106,7 +127,7 @@
         lambda c: og_ref[:, c].astype(f32) * q_ref[:, c].astype(f32),
     )
     pl.semaphore_wait(barrier, devices - 1)
-    send_all(devices, sub, me, out_buf, in_buf, out_send, out_recv)
+    send_all(peers, me, out_buf, in_buf, out_send, out_recv)
     in_buf[me] = out_buf[me]
 
     speed_row = jnp.exp(rate_ref[...])
@@ -132,7 +153,7 @@
             toep[rows, : row * LANES] = jnp.zeros((LANES, row * LANES), bf16)
         toep[rows, row * LANES :] = near[:, : width - row * LANES]
 
-    whole(devices, sub, me, out_buf, in_buf, out_send, out_recv).wait_recv()
+    whole(peers, out_buf, in_buf, out_send, out_recv).wait_recv()
     stage[...] = in_buf[...].reshape(devices * slab, LANES).astype(f32)
 
     def gathered(start):
@@ -152,7 +173,7 @@
     corr = lax.dot_general(gated, toep[...], NT, preferred_element_type=f32)
     corr = corr + jnp.dot(after.astype(bf16), from_after, preferred_element_type=f32)
     back_buf[...] = spread(lambda c: conv[:, c], lambda c: corr[:, c])
-    send_all(devices, sub, me, back_buf, home_buf, back_send, back_recv)
+    send_all(peers, me, back_buf, home_buf, back_send, back_recv)
     home_buf[me] = back_buf[me]
 
     pairs = lax.dot_general(mixed, gated, TN, preferred_element_type=f32)
@@ -191,14 +212,14 @@
     row_ref[0:1, modes : 2 * modes] = -res_row * speed_row * timed * (1.0 / seq_len**0.5)
     row_ref[0:1, 2 * modes : 2 * modes + 1] = skip_sum
 
-    whole(devices, sub, me, back_buf, home_buf, back_send, back_recv).wait_recv()
+    whole(peers, back_buf, home_buf, back_send, back_recv).wait_recv()
     stage[...] = home_buf[...].reshape(channels * slab, LANES).astype(f32)
     for j in range(blocks):
         cols = slice(j * LANES, (j + 1) * LANES)
         conv_ref[:, cols] = stage[pl.ds(j, channels, stride=slab), :].astype(bf16)
         corr_ref[:, cols] = stage[pl.ds(blocks + j, channels, stride=slab), :].astype(bf16)
-    whole(devices, sub, me, out_buf, in_buf, out_send, out_recv).wait_send()
-    whole(devices, sub, me, back_buf, home_buf, back_send, back_recv).wait_send()
+    whole(peers, out_buf, in_buf, out_send, out_recv).wait_send()
+    whole(peers, back_buf, home_buf, back_send, back_recv).wait_send()
 
 
 def finish_kernel(
@@ -232,18 +253,23 @@
     f32, bf16 = jnp.float32, jnp.bfloat16
     vmem = pl.BlockSpec(memory_space=pltpu.VMEM)
     wide = jax.ShapeDtypeStruct((channels, width), bf16)
-    conv, corr, row = pl.pallas_call(
+    gain_row = jax.ShapeDtypeStruct((1, LANES), f32)
+    hbm = pl.BlockSpec(memory_space=pltpu.HBM)
+    conv, corr, row, *loaded = pl.pallas_call(
         functools.partial(exchange_kernel, devices, sub),
-        out_shape=(wide, wide, jax.ShapeDtypeStruct((1, LANES), f32)),
-        in_specs=[vmem] * 6,
-        out_specs=(vmem,) * 3,
+        out_shape=(wide, wide, gain_row, wide, wide, wide, wide, gain_row),
+        in_specs=[hbm] * 7,
+        out_specs=(vmem,) * 8,
         scratch_shapes=[
+            pltpu.VMEM((1, modes), f32),
+            pltpu.VMEM((1, modes), f32),
             pltpu.VMEM((channels * slab, LANES), f32),
             pltpu.VMEM((width, width), bf16),
             pltpu.VMEM((channels, slab, LANES), bf16),
             pltpu.VMEM((devices, slab, LANES), bf16),
             pltpu.VMEM((devices, slab, LANES), bf16),
             pltpu.VMEM((channels, slab, LANES), bf16),
+            pltpu.SemaphoreType.DMA((7,)),
             pltpu.SemaphoreType.DMA,
             pltpu.SemaphoreType.DMA,
             pltpu.SemaphoreType.DMA,
@@ -253,7 +279,7 @@
             collective_id=0, has_side_effects=True, vmem_limit_bytes=32 * 2**20
         ),
         name="exchange",
-    )(queries, key_branch, value_branch, out_grad, residue, log_rate)
+    )(*[pltpu.with_memory_space_constraint(x, pltpu.HBM) for x in (queries, key_branch, value_branch, out_grad, residue, log_rate, skip_gain[None, :])])
     output, grad_query, grad_key, grad_value, grad_residue, grad_rate, grad_skip = pl.pallas_call(
         finish_kernel,
         out_shape=(wide,) * 4
@@ -263,7 +289,7 @@
         out_specs=(vmem,) * 7,
         compiler_params=pltpu.CompilerParams(vmem_limit_bytes=32 * 2**20),
         name="finish",
-    )(queries, key_branch, value_branch, out_grad, skip_gain[None, :], conv, corr, row)
+    )(*loaded, conv, corr, row)
     return (
         output, grad_query, grad_key, grad_value, grad_residue, grad_rate, grad_skip.reshape(1)
     )

time: 34.9 us -> 27 us (0.77)
  local copies, waits for them, and re-layouts: 4.92 us -> 0 us
  Pallas kernels: 29.1 us -> 26.2 us
    unnamed x14 -> x0, local copies, waits for them, and re-layouts: 4.92 us -> none
    pallas_call x1, Pallas kernels: 28.1 us -> 25.2 us  [body(): pl.pallas_call(functools.partial(exchange_kernel, devices, sub), out_shap...]
where the time goes in v2:
time: 27 us; the launch traced here: 26.9 us
  Pallas kernels  26.2 us (97%)
  between operations  0.64 us (2%)
    pallas_call x1, Pallas kernels, body(): pl.pallas_call(functools.partial(exchange_kernel, devices, sub), out_shap...  25.2 us
    pallas_call x1, Pallas kernels, body(): pl.pallas_call(finish_kernel, out_shape=(wide,) * 4 + (jax.ShapeDtypeStru...  1.04 us

profile of v2, /device:TPU:1, one launch (start us, length us, event | category | flops | bytes accessed | tf_op | source)
XLA Modules:
  0.0 26.9 jit_solution(4239951709950928663)
XLA Ops:
  0.6 25.2 %exchange.1 = (bf16[128,512]{1,0:T(8,128)(2,1)S(1)}, bf16[128,512]{1,0:T(8,128)(2,1)S(1)}, f32[1,128]{1,0:T(1,128)S(1)}, bf16[128,512]{1,0:T(8,128)(2,1)S(1)}, b...) custom-call(bf16[128,512]{1,0:T(8,128)(2,1)} %q_hbm.1, ...), custom_call_target="tpu_custom_call" | custom-call | tf_op jit(solution)/shard_map/exchange/pallas_call | solution.py:258
  25.8 1.0 %finish.1 = (bf16[128,512]{1,0:T(8,128)(2,1)}, bf16[128,512]{1,0:T(8,128)(2,1)}, bf16[128,512]{1,0:T(8,128)(2,1)}, bf16[128,512]{1,0:T(8,128)(2,1)}, f32[1,16]{1...) custom-call(bf16[128,512]{1,0:T(8,128)(2,1)S(1)} %get-tuple-element.22.q_ref, ...), custom_call_target="tpu_custom_call" | custom-call | tf_op jit(solution)/shard_map/finish/pallas_call | solution.py:283

commit v3 on v2

--- a/solution.py
+++ b/solution.py
@@ -12,6 +12,7 @@
 NT = (((1,), (1,)), ((), ()))
 TN = (((0,), (0,)), ((), ()))
 LANES = 128
+GROUPS = 8
 
 
 def iota(shape, axis):
@@ -65,9 +66,10 @@
 
 def send_all(peers, me, src, dst, send_sem, recv_sem):
     for peer, place in peers:
+        row = 0 if src.shape[0] == 1 else peer
         pltpu.make_async_remote_copy(
-            src_ref=src.at[peer],
-            dst_ref=dst.at[me],
+            src_ref=src.at[pl.ds(row, 1)],
+            dst_ref=dst.at[pl.ds(me, 1)],
             send_sem=send_sem,
             recv_sem=recv_sem,
             device_id=place,
@@ -75,9 +77,9 @@
         ).start()
 
 
-def whole(peers, src, dst, send_sem, recv_sem):
+def whole(peers, dst, send_sem, recv_sem):
     return pltpu.make_async_remote_copy(
-        src_ref=src.at[pl.ds(0, len(peers))],
+        src_ref=dst.at[pl.ds(0, len(peers))],
         dst_ref=dst.at[pl.ds(0, len(peers))],
         send_sem=send_sem,
         recv_sem=recv_sem,
@@ -86,17 +88,55 @@
     )
 
 
+def loop_steps(count, unroll, step, carry):
+    def some(i, carry):
+        for j in range(unroll):
+            carry = step(i * unroll + j, carry)
+        return carry
+
+    return lax.fori_loop(0, count // unroll, some, carry)
+
+
+def tile_rows(step):
+    return pl.ds(pl.multiple_of(step * GROUPS, GROUPS), GROUPS)
+
+
+def scan_groups(x_ref, y_ref, steps, decays, gains, backward):
+    def step(i, states):
+        rows = tile_rows(steps - 1 - i if backward else i)
+        x = x_ref[rows, :]
+        states = [a * h + x for a, h in zip(decays, states)]
+        y_ref[rows, :] = sum(g * h for g, h in zip(gains, states))
+        return states
+
+    start = [jnp.zeros((GROUPS, LANES), jnp.float32)] * len(decays)
+    return loop_steps(steps, 4, step, start)
+
+
+def add_states(y_ref, steps, decays, states, backward):
+    def step(i, states):
+        rows = tile_rows(steps - 1 - i if backward else i)
+        states = [a * s for a, s in zip(decays, states)]
+        y_ref[rows, :] = y_ref[rows, :] + sum(states)
+        return states
+
+    loop_steps(steps, 8, step, states)
+
+
 def exchange_kernel(
     devices, sub, q_hbm, k_hbm, v_hbm, og_hbm, res_hbm, rate_hbm, gain_hbm,
     conv_ref, corr_ref, row_ref, q_ref, k_ref, v_ref, og_ref, gain_ref,
-    res_ref, rate_ref, stage, toep, out_buf, in_buf, back_buf, home_buf,
-    load_sems, out_send, out_recv, back_send, back_recv,
+    res_ref, rate_ref, stage, out_buf, in_buf, par_buf, par_all, state_buf, state_all,
+    mixed_t, gated_t, conv_t, corr_t, inner, powers,
+    load_sems, out_send, out_recv, par_send, par_recv, state_send, state_recv,
 ):
     me = lax.axis_index("ctx") * sub + lax.axis_index("sub")
     channels, width = q_ref.shape
     blocks = width // LANES
+    steps = width // GROUPS
     slab = 2 * blocks
     modes = res_ref.shape[1]
+    f32, bf16 = jnp.float32, jnp.bfloat16
     peers = partners(me)
     barrier = pltpu.get_barrier_semaphore()
     for _, place in peers:
@@ -113,27 +153,26 @@
     for load in loads:
         load.wait()
 
-    f32, bf16 = jnp.float32, jnp.bfloat16
-
-    def spread(first, second):
-        for j in range(blocks):
-            cols = slice(j * LANES, (j + 1) * LANES)
-            stage[pl.ds(j, channels, stride=slab), :] = first(cols)
-            stage[pl.ds(blocks + j, channels, stride=slab), :] = second(cols)
-        return stage[...].astype(bf16).reshape(channels, slab, LANES)
-
-    out_buf[...] = spread(
-        lambda c: k_ref[:, c].astype(f32) * v_ref[:, c].astype(f32),
-        lambda c: og_ref[:, c].astype(f32) * q_ref[:, c].astype(f32),
-    )
+    mixed_own = k_ref[...].astype(f32) * v_ref[...].astype(f32)
+    gated_own = og_ref[...].astype(f32) * q_ref[...].astype(f32)
+    for j in range(blocks):
+        cols = slice(j * LANES, (j + 1) * LANES)
+        stage[pl.ds(j, channels, stride=slab), :] = mixed_own[:, cols]
+        stage[pl.ds(blocks + j, channels, stride=slab), :] = gated_own[:, cols]
+    out_buf[...] = stage[...].astype(bf16).reshape(channels, slab, LANES)
+    speed_row = jnp.exp(rate_ref[...])
+    res_row = res_ref[...]
+    par_buf[...] = jnp.zeros((1, LANES), f32)
+    par_buf[:, 0:modes] = speed_row
+    par_buf[:, modes : 2 * modes] = res_row
+
     pl.semaphore_wait(barrier, devices - 1)
     send_all(peers, me, out_buf, in_buf, out_send, out_recv)
+    send_all(peers, me, par_buf, par_all, par_send, par_recv)
     in_buf[me] = out_buf[me]
-
-    speed_row = jnp.exp(rate_ref[...])
-    res_row = res_ref[...]
+    par_all[pl.ds(me, 1), :] = par_buf[...]
+
     speed = column(speed_row)
-    res = column(res_row)
     pos = iota((modes, width), 1).astype(f32)
     rise = jnp.exp(-speed * pos)
     fall = jnp.exp(-speed * (width - 1.0 - pos))
@@ -141,19 +180,19 @@
     to_end_timed = (fall * (width - 1.0 - pos)).astype(bf16)
     to_start = rise.astype(bf16)
     to_start_timed = (rise * pos).astype(bf16)
-    from_before = (res * jnp.exp(-speed * (pos + 1.0))).astype(bf16)
-    from_after = (res * jnp.exp(-speed * (width - pos))).astype(bf16)
     grow = jnp.exp(speed * iota((modes, LANES), 1).astype(f32))
-    lag = iota((LANES, width), 1) - iota((LANES, width), 0)
-    near = lax.dot_general(grow, res * rise, TN, precision=FULL, preferred_element_type=f32)
-    near = jnp.where(lag >= 0, near, 0.0).astype(bf16)
-    for row in range(blocks):
-        rows = slice(row * LANES, (row + 1) * LANES)
-        if row:
-            toep[rows, : row * LANES] = jnp.zeros((LANES, row * LANES), bf16)
-        toep[rows, row * LANES :] = near[:, : width - row * LANES]
-
-    whole(peers, out_buf, in_buf, out_send, out_recv).wait_recv()
+    mixed_own = (k_ref[...].astype(f32) * v_ref[...].astype(f32)).astype(bf16).astype(f32)
+    gated_own = (og_ref[...].astype(f32) * q_ref[...].astype(f32)).astype(bf16).astype(f32)
+    per_block = LANES // steps
+    for own, turned in ((mixed_own, mixed_t), (gated_own, gated_t)):
+        for j in range(blocks):
+            block = own[:, j * LANES : (j + 1) * LANES].T
+            for g in range(per_block):
+                turned[pl.ds(j * per_block + g, steps, stride=GROUPS), :] = block[
+                    g * steps : (g + 1) * steps, :
+                ]
+
+    whole(peers, in_buf, out_send, out_recv).wait_recv()
     stage[...] = in_buf[...].reshape(devices * slab, LANES).astype(f32)
 
     def gathered(start):
@@ -168,15 +207,36 @@
     ends, starts = state(mixed, to_end), state(gated, to_start)
     before = running(ends, speed_row, width, 1)
     after = running(starts, speed_row, width, -1)
-    conv = jnp.dot(mixed, toep[...], preferred_element_type=f32)
-    conv = conv + jnp.dot(before.astype(bf16), from_before, preferred_element_type=f32)
-    corr = lax.dot_general(gated, toep[...], NT, preferred_element_type=f32)
-    corr = corr + jnp.dot(after.astype(bf16), from_after, preferred_element_type=f32)
-    back_buf[...] = spread(lambda c: conv[:, c], lambda c: corr[:, c])
-    send_all(peers, me, back_buf, home_buf, back_send, back_recv)
-    home_buf[me] = back_buf[me]
+    state_buf[:, 0:modes] = before
+    state_buf[:, modes : 2 * modes] = after
+    send_all(peers, me, state_buf, state_all, state_send, state_recv)
+    state_all[pl.ds(me, 1), :] = state_buf[pl.ds(me, 1), :]
+
+    whole(peers, par_all, par_send, par_recv).wait_recv()
+    params = par_all[...].T
+    speeds = [jnp.broadcast_to(params[r : r + 1, :], (GROUPS, LANES)) for r in range(modes)]
+    gains = [
+        jnp.broadcast_to(params[modes + r : modes + r + 1, :], (GROUPS, LANES))
+        for r in range(modes)
+    ]
+    decays = [jnp.exp(-x) for x in speeds]
+    group = iota((GROUPS, LANES), 0)
+    for backward, x_ref, y_ref in ((False, mixed_t, conv_t), (True, gated_t, corr_t)):
+        found = scan_groups(x_ref, y_ref, steps, decays, gains, backward)
+        for r in range(modes):
+            sums = found[r]
+            sign = -1 if backward else 1
+            step = 1
+            while step < GROUPS:
+                sums = sums + jnp.exp(-speeds[r] * float(steps * step)) * shifted(sums, sign * step)
+                step *= 2
+            at = backward * modes + r
+            inner[at] = gains[r] * shifted(sums, sign)
+            away = (GROUPS - 1 - group) if backward else group
+            powers[at] = gains[r] * jnp.exp(-speeds[r] * (away * steps).astype(f32))
 
     pairs = lax.dot_general(mixed, gated, TN, preferred_element_type=f32)
+    lag = iota((LANES, width), 1) - iota((LANES, width), 0)
     lagged = []
     for k in range(blocks):
         total = pairs[:LANES, k * LANES : (k + 1) * LANES]
@@ -212,14 +272,22 @@
     row_ref[0:1, modes : 2 * modes] = -res_row * speed_row * timed * (1.0 / seq_len**0.5)
     row_ref[0:1, 2 * modes : 2 * modes + 1] = skip_sum
 
-    whole(peers, back_buf, home_buf, back_send, back_recv).wait_recv()
-    stage[...] = home_buf[...].reshape(channels * slab, LANES).astype(f32)
-    for j in range(blocks):
-        cols = slice(j * LANES, (j + 1) * LANES)
-        conv_ref[:, cols] = stage[pl.ds(j, channels, stride=slab), :].astype(bf16)
-        corr_ref[:, cols] = stage[pl.ds(blocks + j, channels, stride=slab), :].astype(bf16)
-    whole(peers, out_buf, in_buf, out_send, out_recv).wait_send()
-    whole(peers, back_buf, home_buf, back_send, back_recv).wait_send()
+    whole(peers, state_all, state_send, state_recv).wait_recv()
+    states = state_all[...].T
+    for backward, y_ref, to_ref in ((False, conv_t, conv_ref), (True, corr_t, corr_ref)):
+        start = []
+        for r in range(modes):
+            at = backward * modes + r
+            start.append(inner[at] + powers[at] * states[at : at + 1, :])
+        add_states(y_ref, steps, decays, start, backward)
+        for j in range(blocks):
+            parts = [
+                y_ref[pl.ds(j * per_block + g, steps, stride=GROUPS), :] for g in range(per_block)
+            ]
+            to_ref[:, j * LANES : (j + 1) * LANES] = jnp.concatenate(parts, axis=0).T
+    whole(peers, in_buf, out_send, out_recv).wait_send()
+    whole(peers, par_all, par_send, par_recv).wait_send()
+    whole(peers, state_all, state_send, state_recv).wait_send()
 
 
 def finish_kernel(
@@ -233,8 +301,8 @@
     v, og = v_ref[...].astype(f32), og_ref[...].astype(f32)
     mixed = (k * v).astype(bf16).astype(f32)
     gated = (og * q).astype(bf16).astype(f32)
-    forward_sum = conv_ref[...].astype(f32) + gain * mixed
-    input_grad = corr_ref[...].astype(f32) + gain * gated
+    forward_sum = conv_ref[...] + gain * mixed
+    input_grad = corr_ref[...] + gain * gated
     out_ref[...] = (q * forward_sum).astype(bf16)
     gq_ref[...] = (og * forward_sum).astype(bf16)
     gk_ref[...] = (input_grad * v).astype(bf16)
@@ -253,23 +321,33 @@
     f32, bf16 = jnp.float32, jnp.bfloat16
     vmem = pl.BlockSpec(memory_space=pltpu.VMEM)
     wide = jax.ShapeDtypeStruct((channels, width), bf16)
+    full = jax.ShapeDtypeStruct((channels, width), f32)
     gain_row = jax.ShapeDtypeStruct((1, LANES), f32)
     hbm = pl.BlockSpec(memory_space=pltpu.HBM)
     conv, corr, row, *loaded = pl.pallas_call(
         functools.partial(exchange_kernel, devices, sub),
-        out_shape=(wide, wide, gain_row, wide, wide, wide, wide, gain_row),
+        out_shape=(full, full, gain_row, wide, wide, wide, wide, gain_row),
         in_specs=[hbm] * 7,
         out_specs=(vmem,) * 8,
         scratch_shapes=[
             pltpu.VMEM((1, modes), f32),
             pltpu.VMEM((1, modes), f32),
             pltpu.VMEM((channels * slab, LANES), f32),
-            pltpu.VMEM((width, width), bf16),
             pltpu.VMEM((channels, slab, LANES), bf16),
             pltpu.VMEM((devices, slab, LANES), bf16),
-            pltpu.VMEM((devices, slab, LANES), bf16),
-            pltpu.VMEM((channels, slab, LANES), bf16),
+            pltpu.VMEM((1, LANES), f32),
+            pltpu.VMEM((channels, LANES), f32),
+            pltpu.VMEM((devices, LANES), f32),
+            pltpu.VMEM((channels, LANES), f32),
+            pltpu.VMEM((width, LANES), f32),
+            pltpu.VMEM((width, LANES), f32),
+            pltpu.VMEM((width, LANES), f32),
+            pltpu.VMEM((width, LANES), f32),
+            pltpu.VMEM((2 * modes, GROUPS, LANES), f32),
+            pltpu.VMEM((2 * modes, GROUPS, LANES), f32),
             pltpu.SemaphoreType.DMA((7,)),
+            pltpu.SemaphoreType.DMA,
+            pltpu.SemaphoreType.DMA,
             pltpu.SemaphoreType.DMA,
             pltpu.SemaphoreType.DMA,
             pltpu.SemaphoreType.DMA,

time: 27 us -> 26.4 us (0.978)
  Pallas kernels: 26.2 us -> 25.7 us
    pallas_call x1, Pallas kernels: 25.2 us -> 24.7 us  [body(): pl.pallas_call(functools.partial(exchange_kernel, devices, sub), out_shap...]
where the time goes in v3:
time: 26.4 us; the launch traced here: 26.3 us
  Pallas kernels  25.7 us (97%)
  between operations  0.64 us (2%)
    pallas_call x1, Pallas kernels, body(): pl.pallas_call(functools.partial(exchange_kernel, devices, sub), out_shap...  24.7 us
    pallas_call x1, Pallas kernels, body(): pl.pallas_call(finish_kernel, out_shape=(wide,) * 4 + (jax.ShapeDtypeStru...  1.01 us

profile of v3, /device:TPU:1, one launch (start us, length us, event | category | flops | bytes accessed | tf_op | source)
XLA Modules:
  0.0 26.3 jit_solution(15816897998763739207)
XLA Ops:
  0.6 24.7 %exchange.1 = (f32[128,512]{1,0:T(8,128)S(1)}, f32[128,512]{1,0:T(8,128)S(1)}, f32[1,128]{1,0:T(1,128)S(1)}, bf16[128,512]{1,0:T(8,128)(2,1)S(1)}, bf16[128,512]...) custom-call(bf16[128,512]{1,0:T(8,128)(2,1)} %q_hbm.1, ...), custom_call_target="tpu_custom_call" | custom-call | tf_op jit(solution)/shard_map/exchange/pallas_call | solution.py:327
  25.3 1.0 %finish.1 = (bf16[128,512]{1,0:T(8,128)(2,1)}, bf16[128,512]{1,0:T(8,128)(2,1)}, bf16[128,512]{1,0:T(8,128)(2,1)}, bf16[128,512]{1,0:T(8,128)(2,1)}, f32[1,16]{1...) custom-call(bf16[128,512]{1,0:T(8,128)(2,1)S(1)} %get-tuple-element.22.q_ref, ...), custom_call_target="tpu_custom_call" | custom-call | tf_op jit(solution)/shard_map/finish/pallas_call | solution.py:361

commit v4 on v3

--- a/solution.py
+++ b/solution.py
@@ -23,6 +23,12 @@
     n = row.shape[1]
     eye = iota((n, n), 0) == iota((n, n), 1)
     return jnp.sum(jnp.where(eye, row, 0.0), axis=1, keepdims=True)
+
+
+def as_row(col):
+    n = col.shape[0]
+    eye = iota((n, n), 0) == iota((n, n), 1)
+    return jnp.sum(jnp.where(eye, col, 0.0), axis=0, keepdims=True)
 
 
 def shifted(rows, count):
@@ -123,11 +129,19 @@
     loop_steps(steps, 8, step, states)
 
 
+def natural(y_ref, steps, j):
+    per_block = LANES // steps
+    parts = [
+        y_ref[pl.ds(j * per_block + g, steps, stride=GROUPS), :] for g in range(per_block)
+    ]
+    return jnp.concatenate(parts, axis=0).T
+
+
 def exchange_kernel(
     devices, sub, q_hbm, k_hbm, v_hbm, og_hbm, res_hbm, rate_hbm, gain_hbm,
-    conv_ref, corr_ref, row_ref, q_ref, k_ref, v_ref, og_ref, gain_ref,
-    res_ref, rate_ref, stage, out_buf, in_buf, par_buf, par_all, state_buf, state_all,
-    mixed_t, gated_t, conv_t, corr_t, inner, powers,
+    sum_ref, grad_ref, row_ref, q_ref, k_ref, v_ref, og_ref, state_ref, factor_ref, rise_ref,
+    fall_ref, gain_ref, res_ref, rate_ref, stage, out_buf, in_buf, par_buf, par_all, state_buf, state_all,
+    mixed_t, gated_t, conv_t, corr_t,
     load_sems, out_send, out_recv, par_send, par_recv, state_send, state_recv,
 ):
     me = lax.axis_index("ctx") * sub + lax.axis_index("sub")
@@ -173,12 +187,16 @@
     par_all[pl.ds(me, 1), :] = par_buf[...]
 
     speed = column(speed_row)
+    copies = LANES // modes
+    half = copies // 2
+    wide_speed = as_row(jnp.concatenate([speed] * copies, axis=0))
     pos = iota((modes, width), 1).astype(f32)
     rise = jnp.exp(-speed * pos)
     fall = jnp.exp(-speed * (width - 1.0 - pos))
-    to_end = fall.astype(bf16)
+    blank = jnp.zeros((half * modes, width), f32)
+    to_end = jnp.concatenate([fall] * half + [blank], axis=0).astype(bf16)
+    to_start = jnp.concatenate([blank] + [rise] * half, axis=0).astype(bf16)
     to_end_timed = (fall * (width - 1.0 - pos)).astype(bf16)
-    to_start = rise.astype(bf16)
     to_start_timed = (rise * pos).astype(bf16)
     grow = jnp.exp(speed * iota((modes, LANES), 1).astype(f32))
     mixed_own = (k_ref[...].astype(f32) * v_ref[...].astype(f32)).astype(bf16).astype(f32)
@@ -205,10 +223,9 @@
         return lax.dot_general(rows, weights, NT, preferred_element_type=f32)
 
     ends, starts = state(mixed, to_end), state(gated, to_start)
-    before = running(ends, speed_row, width, 1)
-    after = running(starts, speed_row, width, -1)
-    state_buf[:, 0:modes] = before
-    state_buf[:, modes : 2 * modes] = after
+    before = running(ends, wide_speed, width, 1)
+    after = running(starts, wide_speed, width, -1)
+    state_buf[...] = before + after
     send_all(peers, me, state_buf, state_all, state_send, state_recv)
     state_all[pl.ds(me, 1), :] = state_buf[pl.ds(me, 1), :]
 
@@ -220,20 +237,46 @@
         for r in range(modes)
     ]
     decays = [jnp.exp(-x) for x in speeds]
-    group = iota((GROUPS, LANES), 0)
-    for backward, x_ref, y_ref in ((False, mixed_t, conv_t), (True, gated_t, corr_t)):
+    gain = column(gain_ref[...])
+    for backward, own, x_ref, y_ref, to_ref in (
+        (False, mixed_own, mixed_t, conv_t, sum_ref), (True, gated_own, gated_t, corr_t, grad_ref)
+    ):
         found = scan_groups(x_ref, y_ref, steps, decays, gains, backward)
+        sign = -1 if backward else 1
+        inner = []
         for r in range(modes):
             sums = found[r]
-            sign = -1 if backward else 1
             step = 1
             while step < GROUPS:
                 sums = sums + jnp.exp(-speeds[r] * float(steps * step)) * shifted(sums, sign * step)
                 step *= 2
-            at = backward * modes + r
-            inner[at] = gains[r] * shifted(sums, sign)
-            away = (GROUPS - 1 - group) if backward else group
-            powers[at] = gains[r] * jnp.exp(-speeds[r] * (away * steps).astype(f32))
+            inner.append(gains[r] * shifted(sums, sign))
+        add_states(y_ref, steps, decays, inner, backward)
+        for j in range(blocks):
+            cols = slice(j * LANES, (j + 1) * LANES)
+            to_ref[:, cols] = natural(y_ref, steps, j) + gain * own[:, cols]
+
+    lane = iota((channels, LANES), 1)
+    own_gain = jnp.where((lane >= modes) & (lane < 2 * modes), par_all[...], 0.0)
+    own_gain = pltpu.roll(own_gain, LANES - modes, 1)
+    own_speed = jnp.where(lane < modes, par_all[...], 0.0)
+    step = modes
+    while step < LANES:
+        own_gain = own_gain + pltpu.roll(own_gain, step, 1)
+        own_speed = own_speed + pltpu.roll(own_speed, step, 1)
+        step *= 2
+    home = iota((channels, LANES), 0) % (2 * copies) - lane // modes
+    for n in range(blocks):
+        scaled = own_gain * jnp.exp(-own_speed * float(n * LANES))
+        factor_ref[n, :, :LANES] = jnp.where(home == 0, scaled, 0.0)
+        factor_ref[n, :, LANES:] = jnp.where(home == copies, scaled, 0.0)
+    ahead = (iota((modes, LANES), 1) + 1).astype(f32)
+    behind = (LANES - iota((modes, LANES), 1)).astype(f32)
+    for c in range(channels):
+        rate = -params[:modes, c : c + 1]
+        rows = slice(c * modes, (c + 1) * modes)
+        rise_ref[rows, :] = jnp.exp(rate * ahead).astype(bf16)
+        fall_ref[rows, :] = jnp.exp(rate * behind).astype(bf16)
 
     pairs = lax.dot_general(mixed, gated, TN, preferred_element_type=f32)
     lag = iota((LANES, width), 1) - iota((LANES, width), 0)
@@ -253,14 +296,11 @@
 
     plain_col = local_sum(lagged)
     timed_col = local_sum(lagged * lag.astype(f32))
-    eye = iota((modes, modes), 0) == iota((modes, modes), 1)
-
-    def as_row(col):
-        return jnp.sum(jnp.where(eye, col, 0.0), axis=0, keepdims=True)
-
     one_step = jnp.exp(-speed_row)
     chunk_step = jnp.exp(-speed_row * float(width))
     ends_timed, starts_timed = state(mixed, to_end_timed), state(gated, to_start_timed)
+    first, second = slice(0, modes), slice(half * modes, (half + 1) * modes)
+    before, after, starts = before[:, first], after[:, second], starts[:, second]
     cross = before * starts
     cross_timed = ends_timed * after + before * starts_timed + cross
     cross_timed = cross_timed + (float(width) * chunk_step) * (before * after)
@@ -272,44 +312,50 @@
     row_ref[0:1, modes : 2 * modes] = -res_row * speed_row * timed * (1.0 / seq_len**0.5)
     row_ref[0:1, 2 * modes : 2 * modes + 1] = skip_sum
 
-    whole(peers, state_all, state_send, state_recv).wait_recv()
-    states = state_all[...].T
-    for backward, y_ref, to_ref in ((False, conv_t, conv_ref), (True, corr_t, corr_ref)):
-        start = []
-        for r in range(modes):
-            at = backward * modes + r
-            start.append(inner[at] + powers[at] * states[at : at + 1, :])
-        add_states(y_ref, steps, decays, start, backward)
-        for j in range(blocks):
-            parts = [
-                y_ref[pl.ds(j * per_block + g, steps, stride=GROUPS), :] for g in range(per_block)
-            ]
-            to_ref[:, j * LANES : (j + 1) * LANES] = jnp.concatenate(parts, axis=0).T
     whole(peers, in_buf, out_send, out_recv).wait_send()
     whole(peers, par_all, par_send, par_recv).wait_send()
+    whole(peers, state_all, state_send, state_recv).wait_recv()
+    state_ref[...] = state_all[...]
     whole(peers, state_all, state_send, state_recv).wait_send()
 
 
 def finish_kernel(
-    q_ref, k_ref, v_ref, og_ref, gain_ref, conv_ref, corr_ref, row_ref,
-    out_ref, gq_ref, gk_ref, gv_ref, gres_ref, grate_ref, gskip_ref,
+    q_ref, k_ref, v_ref, og_ref, sum_ref, grad_ref, row_ref, state_ref, factor_ref, rise_ref,
+    fall_ref, out_ref, gq_ref, gk_ref, gv_ref, gres_ref, grate_ref, gskip_ref,
 ):
     f32, bf16 = jnp.float32, jnp.bfloat16
+    channels, width = q_ref.shape
     modes = gres_ref.shape[1]
-    gain = column(gain_ref[...])
-    q, k = q_ref[...].astype(f32), k_ref[...].astype(f32)
-    v, og = v_ref[...].astype(f32), og_ref[...].astype(f32)
-    mixed = (k * v).astype(bf16).astype(f32)
-    gated = (og * q).astype(bf16).astype(f32)
-    forward_sum = conv_ref[...] + gain * mixed
-    input_grad = corr_ref[...] + gain * gated
-    out_ref[...] = (q * forward_sum).astype(bf16)
-    gq_ref[...] = (og * forward_sum).astype(bf16)
-    gk_ref[...] = (input_grad * v).astype(bf16)
-    gv_ref[...] = (input_grad * k).astype(bf16)
+    copies = LANES // modes
     gres_ref[...] = row_ref[:, 0:modes]
     grate_ref[...] = row_ref[:, modes : 2 * modes]
     gskip_ref[...] = row_ref[:, 2 * modes : 2 * modes + 1]
+    blocks = width // LANES
+    tall = 2 * copies
+    states = state_ref[...]
+    other = pltpu.roll(states, LANES // 2, 1)
+    first = iota((channels, LANES), 1) < LANES // 2
+    before = jnp.where(first, states, other)
+    after = jnp.where(first, other, states)
+    for g in range(channels // tall):
+        rows = slice(g * tall, (g + 1) * tall)
+        deep = slice(g * tall * modes, (g + 1) * tall * modes)
+        for found, order, table_ref, base_ref, pair, places in (
+            (before, 1, rise_ref, sum_ref, (q_ref, og_ref), (out_ref, gq_ref)),
+            (after, -1, fall_ref, grad_ref, (v_ref, k_ref), (gk_ref, gv_ref)),
+        ):
+            own = jnp.concatenate([found[rows, :]] * 2, axis=1)
+            parts = [own * factor_ref[n, rows, :] for n in range(blocks)][::order]
+            share = jnp.dot(
+                jnp.concatenate(parts, axis=0).astype(bf16),
+                table_ref[deep, :],
+                preferred_element_type=f32,
+            )
+            for n in range(blocks):
+                cols = slice(n * LANES, (n + 1) * LANES)
+                total = share[n * tall : (n + 1) * tall, :] + base_ref[rows, cols]
+                for factor, place in zip(pair, places):
+                    place[rows, cols] = (factor[rows, cols].astype(f32) * total).astype(bf16)
 
 
 def body(queries, key_branch, value_branch, out_grad, residue, log_rate, skip_gain):
@@ -322,14 +368,21 @@
     vmem = pl.BlockSpec(memory_space=pltpu.VMEM)
     wide = jax.ShapeDtypeStruct((channels, width), bf16)
     full = jax.ShapeDtypeStruct((channels, width), f32)
-    gain_row = jax.ShapeDtypeStruct((1, LANES), f32)
+    square = jax.ShapeDtypeStruct((channels, LANES), f32)
+    table = jax.ShapeDtypeStruct((channels * modes, LANES), bf16)
+    factors = jax.ShapeDtypeStruct((width // LANES, channels, 2 * LANES), f32)
     hbm = pl.BlockSpec(memory_space=pltpu.HBM)
-    conv, corr, row, *loaded = pl.pallas_call(
+    operands = (queries, key_branch, value_branch, out_grad, residue, log_rate, skip_gain[None, :])
+    total, grad, row, q, k, v, og, *states = pl.pallas_call(
         functools.partial(exchange_kernel, devices, sub),
-        out_shape=(full, full, gain_row, wide, wide, wide, wide, gain_row),
+        out_shape=(
+            full, full, jax.ShapeDtypeStruct((1, LANES), f32), wide, wide, wide, wide,
+            square, factors, table, table,
+        ),
         in_specs=[hbm] * 7,
-        out_specs=(vmem,) * 8,
+        out_specs=(vmem,) * 11,
         scratch_shapes=[
+            pltpu.VMEM((1, channels), f32),
             pltpu.VMEM((1, modes), f32),
             pltpu.VMEM((1, modes), f32),
             pltpu.VMEM((channels * slab, LANES), f32),
@@ -343,8 +396,6 @@
             pltpu.VMEM((width, LANES), f32),
             pltpu.VMEM((width, LANES), f32),
             pltpu.VMEM((width, LANES), f32),
-            pltpu.VMEM((2 * modes, GROUPS, LANES), f32),
-            pltpu.VMEM((2 * modes, GROUPS, LANES), f32),
             pltpu.SemaphoreType.DMA((7,)),
             pltpu.SemaphoreType.DMA,
             pltpu.SemaphoreType.DMA,
@@ -357,17 +408,17 @@
             collective_id=0, has_side_effects=True, vmem_limit_bytes=32 * 2**20
         ),
         name="exchange",
-    )(*[pltpu.with_memory_space_constraint(x, pltpu.HBM) for x in (queries, key_branch, value_branch, out_grad, residue, log_rate, skip_gain[None, :])])
+    )(*[pltpu.with_memory_space_constraint(x, pltpu.HBM) for x in operands])
     output, grad_query, grad_key, grad_value, grad_residue, grad_rate, grad_skip = pl.pallas_call(
         finish_kernel,
         out_shape=(wide,) * 4
         + (jax.ShapeDtypeStruct((1, modes), f32),) * 2
         + (jax.ShapeDtypeStruct((1, 1), f32),),
-        in_specs=[vmem] * 8,
+        in_specs=[vmem] * 11,
         out_specs=(vmem,) * 7,
         compiler_params=pltpu.CompilerParams(vmem_limit_bytes=32 * 2**20),
         name="finish",
-    )(*loaded, conv, corr, row)
+    )(q, k, v, og, total, grad, row, *states)
     return (
         output, grad_query, grad_key, grad_value, grad_residue, grad_rate, grad_skip.reshape(1)
     )

time: 26.4 us -> 25.5 us (0.966)
  Pallas kernels: 25.7 us -> 24.7 us
    pallas_call x1, Pallas kernels: 24.7 us -> 23.5 us  [body(): pl.pallas_call(functools.partial(exchange_kernel, devices, sub), out_shap...]
where the time goes in v4:
time: 25.5 us; the launch traced here: 25.3 us
  Pallas kernels  24.7 us (97%)
  between operations  0.64 us (3%)
    pallas_call x1, Pallas kernels, body(): pl.pallas_call(functools.partial(exchange_kernel, devices, sub), out_shap...  23.5 us
    pallas_call x1, Pallas kernels, body(): pl.pallas_call(finish_kernel, out_shape=(wide,) * 4 + (jax.ShapeDtypeStru...  1.16 us

profile of v4, /device:TPU:1, one launch (start us, length us, event | category | flops | bytes accessed | tf_op | source)
XLA Modules:
  0.0 25.3 jit_solution(13925671697360135190)
XLA Ops:
  0.6 23.5 %exchange.1 = (f32[128,512]{1,0:T(8,128)S(1)}, f32[128,512]{1,0:T(8,128)S(1)}, f32[1,128]{1,0:T(1,128)S(1)}, bf16[128,512]{1,0:T(8,128)(2,1)S(1)}, bf16[128,512]...) custom-call(bf16[128,512]{1,0:T(8,128)(2,1)} %q_hbm.1, ...), custom_call_target="tpu_custom_call" | custom-call | tf_op jit(solution)/shard_map/exchange/pallas_call | solution.py:376
  24.2 1.2 %finish.1 = (bf16[128,512]{1,0:T(8,128)(2,1)}, bf16[128,512]{1,0:T(8,128)(2,1)}, bf16[128,512]{1,0:T(8,128)(2,1)}, bf16[128,512]{1,0:T(8,128)(2,1)}, f32[1,16]{1...) custom-call(bf16[128,512]{1,0:T(8,128)(2,1)S(1)} %get-tuple-element.25.q_ref, ...), custom_call_target="tpu_custom_call" | custom-call | tf_op jit(solution)/shard_map/finish/pallas_call | solution.py:412

commit v5 on v4

--- a/solution.py
+++ b/solution.py
@@ -13,6 +13,9 @@
 TN = (((0,), (0,)), ((), ()))
 LANES = 128
 GROUPS = 8
+FAR = (
+    (2, 2, 2), (2, 2, 1), (2, 2, 3), (2, 1, 2), (2, 3, 2), (1, 2, 2), (3, 2, 2), (2, 3, 3), (3, 2, 3)
+)
 
 
 def iota(shape, axis):
@@ -49,9 +52,31 @@
     return shifted(rows, sign)
 
 
-def partners(me):
+def place_of(me):
     core, z = me % 2, me // 4 % 4
     y, x = me // 2 % 2 * 2 + me // 16 % 2, me // 32
+    return x, y, z, core
+
+
+def index_of(x, y, z, core):
+    return x * 32 + y % 2 * 16 + z * 4 + y // 2 * 2 + core
+
+
+def opposite(chip):
+    return tuple((v + 2) % 4 for v in chip)
+
+
+def among(place, chips):
+    x, y, z, _ = place
+    mine = x * 16 + y * 4 + z
+    found = mine < 0
+    for cx, cy, cz in chips:
+        found = jnp.logical_or(found, mine == cx * 16 + cy * 4 + cz)
+    return found
+
+
+def partners(me):
+    x, y, z, core = place_of(me)
     across = [lax.rem(x + d, 4) * 8 for d in range(4)]
     along = [lax.rem(z + d, 4) for d in range(4)]
     ups = [lax.rem(y + d, 4) for d in range(4)]
@@ -70,23 +95,28 @@
     return found
 
 
-def send_all(peers, me, src, dst, send_sem, recv_sem):
+def row_copy(src, row, dst, at, send_sem, recv_sem, place):
+    return pltpu.make_async_remote_copy(
+        src_ref=src.at[pl.ds(row, 1)],
+        dst_ref=dst.at[pl.ds(at, 1)],
+        send_sem=send_sem,
+        recv_sem=recv_sem,
+        device_id=place,
+        device_id_type=MESH,
+    )
+
+
+def send_all(peers, at, src, dst, send_sem, recv_sem):
     for peer, place in peers:
         row = 0 if src.shape[0] == 1 else peer
-        pltpu.make_async_remote_copy(
-            src_ref=src.at[pl.ds(row, 1)],
-            dst_ref=dst.at[pl.ds(me, 1)],
-            send_sem=send_sem,
-            recv_sem=recv_sem,
-            device_id=place,
-            device_id_type=MESH,
-        ).start()
-
-
-def whole(peers, dst, send_sem, recv_sem):
+        row_copy(src, row, dst, at, send_sem, recv_sem, place).start()
+
+
+def whole(peers, dst, send_sem, recv_sem, count=None):
+    count = count or len(peers)
     return pltpu.make_async_remote_copy(
-        src_ref=dst.at[pl.ds(0, len(peers))],
-        dst_ref=dst.at[pl.ds(0, len(peers))],
+        src_ref=dst.at[pl.ds(0, count)],
+        dst_ref=dst.at[pl.ds(0, count)],
         send_sem=send_sem,
         recv_sem=recv_sem,
         device_id=peers[0][1],
@@ -141,8 +171,9 @@
     devices, sub, q_hbm, k_hbm, v_hbm, og_hbm, res_hbm, rate_hbm, gain_hbm,
     sum_ref, grad_ref, row_ref, q_ref, k_ref, v_ref, og_ref, state_ref, factor_ref, rise_ref,
     fall_ref, gain_ref, res_ref, rate_ref, stage, out_buf, in_buf, par_buf, par_all, state_buf, state_all,
-    mixed_t, gated_t, conv_t, corr_t,
+    mixed_t, gated_t, conv_t, corr_t, second_buf, second_par, second_state,
     load_sems, out_send, out_recv, par_send, par_recv, state_send, state_recv,
+    extra_send, extra_recv, ahead_send, ahead_recv, second_send,
 ):
     me = lax.axis_index("ctx") * sub + lax.axis_index("sub")
     channels, width = q_ref.shape
@@ -152,6 +183,10 @@
     modes = res_ref.shape[1]
     f32, bf16 = jnp.float32, jnp.bfloat16
     peers = partners(me)
+    place = place_of(me)
+    far, near = among(place, FAR), among(place, [opposite(chip) for chip in FAR])
+    across = index_of(*[lax.rem(v + 2, 4) for v in place[:3]], place[3])
+    across_place = (across // sub, lax.rem(across, sub))
     barrier = pltpu.get_barrier_semaphore()
     for _, place in peers:
         pl.semaphore_signal(barrier, inc=1, device_id=place, device_id_type=MESH)
@@ -181,21 +216,41 @@
     par_buf[:, modes : 2 * modes] = res_row
 
     pl.semaphore_wait(barrier, devices - 1)
+    row_copy(par_buf, 0, second_par, 0, ahead_send, ahead_recv, across_place).start()
     send_all(peers, me, out_buf, in_buf, out_send, out_recv)
+    for chip in FAR:
+        for core in range(2):
+            src, to = index_of(*chip, core), index_of(*opposite(chip), core)
+
+            @pl.when(me != to)
+            def _(src=src, to=to):
+                row_copy(
+                    out_buf, src, second_buf, me, extra_send, extra_recv, (to // sub, to % sub)
+                ).start()
+
+            @pl.when(me == to)
+            def _(src=src, to=to):
+                second_buf[to] = out_buf[src]
+
     send_all(peers, me, par_buf, par_all, par_send, par_recv)
     in_buf[me] = out_buf[me]
     par_all[pl.ds(me, 1), :] = par_buf[...]
 
-    speed = column(speed_row)
     copies = LANES // modes
     half = copies // 2
-    wide_speed = as_row(jnp.concatenate([speed] * copies, axis=0))
     pos = iota((modes, width), 1).astype(f32)
-    rise = jnp.exp(-speed * pos)
-    fall = jnp.exp(-speed * (width - 1.0 - pos))
     blank = jnp.zeros((half * modes, width), f32)
-    to_end = jnp.concatenate([fall] * half + [blank], axis=0).astype(bf16)
-    to_start = jnp.concatenate([blank] + [rise] * half, axis=0).astype(bf16)
+
+    def weights(speed):
+        rise = jnp.exp(-speed * pos)
+        fall = jnp.exp(-speed * (width - 1.0 - pos))
+        to_end = jnp.concatenate([fall] * half + [blank], axis=0).astype(bf16)
+        to_start = jnp.concatenate([blank] + [rise] * half, axis=0).astype(bf16)
+        wide_speed = as_row(jnp.concatenate([speed] * copies, axis=0))
+        return rise, fall, to_end, to_start, wide_speed
+
+    speed = column(speed_row)
+    rise, fall, to_end, to_start, wide_speed = weights(speed)
     to_end_timed = (fall * (width - 1.0 - pos)).astype(bf16)
     to_start_timed = (rise * pos).astype(bf16)
     grow = jnp.exp(speed * iota((modes, LANES), 1).astype(f32))
@@ -210,24 +265,41 @@
                     g * steps : (g + 1) * steps, :
                 ]
 
-    whole(peers, in_buf, out_send, out_recv).wait_recv()
-    stage[...] = in_buf[...].reshape(devices * slab, LANES).astype(f32)
-
-    def gathered(start):
-        parts = [stage[pl.ds(start + j, devices, stride=slab), :] for j in range(blocks)]
-        return jnp.concatenate(parts, axis=1).astype(bf16)
-
-    mixed, gated = gathered(0), gathered(blocks)
+    row_copy(par_buf, 0, second_par, 0, ahead_send, ahead_recv, across_place).wait_recv()
+    second_weights = weights(column(second_par[:, :modes]))[2:]
 
     def state(rows, weights):
         return lax.dot_general(rows, weights, NT, preferred_element_type=f32)
 
-    ends, starts = state(mixed, to_end), state(gated, to_start)
-    before = running(ends, wide_speed, width, 1)
-    after = running(starts, wide_speed, width, -1)
-    state_buf[...] = before + after
-    send_all(peers, me, state_buf, state_all, state_send, state_recv)
-    state_all[pl.ds(me, 1), :] = state_buf[pl.ds(me, 1), :]
+    def owned(buf, to_end, to_start, wide_speed):
+        stage[...] = buf[...].reshape(devices * slab, LANES).astype(f32)
+
+        def gathered(start):
+            parts = [stage[pl.ds(start + j, devices, stride=slab), :] for j in range(blocks)]
+            return jnp.concatenate(parts, axis=1).astype(bf16)
+
+        mixed, gated = gathered(0), gathered(blocks)
+        ends, starts = state(mixed, to_end), state(gated, to_start)
+        before = running(ends, wide_speed, width, 1)
+        after = running(starts, wide_speed, width, -1)
+        return mixed, gated, starts, before, after
+
+    whole(peers, in_buf, out_send, out_recv).wait_recv()
+    mixed, gated, starts, before, after = owned(in_buf, to_end, to_start, wide_speed)
+
+    @pl.when(jnp.logical_not(far))
+    def _():
+        state_buf[...] = before + after
+        send_all(peers, me, state_buf, state_all, state_send, state_recv)
+        state_all[pl.ds(me, 1), :] = state_buf[pl.ds(me, 1), :]
+
+    @pl.when(near)
+    def _():
+        whole(peers, second_buf, extra_send, extra_recv).wait_recv()
+        *_, before, after = owned(second_buf, *second_weights)
+        second_state[...] = before + after
+        send_all(peers, across, second_state, state_all, second_send, state_recv)
+        state_all[pl.ds(across, 1), :] = second_state[pl.ds(me, 1), :]
 
     whole(peers, par_all, par_send, par_recv).wait_recv()
     params = par_all[...].T
@@ -312,11 +384,34 @@
     row_ref[0:1, modes : 2 * modes] = -res_row * speed_row * timed * (1.0 / seq_len**0.5)
     row_ref[0:1, 2 * modes : 2 * modes + 1] = skip_sum
 
+    extras = 2 * len(FAR)
     whole(peers, in_buf, out_send, out_recv).wait_send()
     whole(peers, par_all, par_send, par_recv).wait_send()
-    whole(peers, state_all, state_send, state_recv).wait_recv()
+    row_copy(par_buf, 0, second_par, 0, ahead_send, ahead_recv, across_place).wait_send()
+
+    @pl.when(near)
+    def _():
+        whole(peers, second_buf, extra_send, extra_recv, extras - 1).wait_send()
+        whole(peers, state_all, state_send, state_recv, devices - 2).wait_recv()
+        whole(peers, state_all, second_send, state_recv).wait_send()
+
+    @pl.when(jnp.logical_not(near))
+    def _():
+        whole(peers, second_buf, extra_send, extra_recv, extras).wait_send()
+
+    @pl.when(far)
+    def _():
+        whole(peers, state_all, state_send, state_recv, devices).wait_recv()
+
+    @pl.when(jnp.logical_not(jnp.logical_or(near, far)))
+    def _():
+        whole(peers, state_all, state_send, state_recv).wait_recv()
+
+    @pl.when(jnp.logical_not(far))
+    def _():
+        whole(peers, state_all, state_send, state_recv).wait_send()
+
     state_ref[...] = state_all[...]
-    whole(peers, state_all, state_send, state_recv).wait_send()
 
 
 def finish_kernel(
@@ -396,7 +491,15 @@
             pltpu.VMEM((width, LANES), f32),
             pltpu.VMEM((width, LANES), f32),
             pltpu.VMEM((width, LANES), f32),
+            pltpu.VMEM((devices, slab, LANES), bf16),
+            pltpu.VMEM((1, LANES), f32),
+            pltpu.VMEM((devices, LANES), f32),
             pltpu.SemaphoreType.DMA((7,)),
+            pltpu.SemaphoreType.DMA,
+            pltpu.SemaphoreType.DMA,
+            pltpu.SemaphoreType.DMA,
+            pltpu.SemaphoreType.DMA,
+            pltpu.SemaphoreType.DMA,
             pltpu.SemaphoreType.DMA,
             pltpu.SemaphoreType.DMA,
             pltpu.SemaphoreType.DMA,

time: 25.5 us -> 28.1 us (1.10)
  Pallas kernels: 24.7 us -> 27.3 us
    pallas_call x1, Pallas kernels: 23.5 us -> 26.1 us  [body(): pl.pallas_call(functools.partial(exchange_kernel, devices, sub), out_shap...]
where the time goes in v5:
time: 28.1 us; the launch traced here: 27.9 us
  Pallas kernels  27.3 us (97%)
  between operations  0.64 us (2%)
    pallas_call x1, Pallas kernels, body(): pl.pallas_call(functools.partial(exchange_kernel, devices, sub), out_shap...  26.1 us
    pallas_call x1, Pallas kernels, body(): pl.pallas_call(finish_kernel, out_shape=(wide,) * 4 + (jax.ShapeDtypeStru...  1.16 us

profile of v5, /device:TPU:1, one launch (start us, length us, event | category | flops | bytes accessed | tf_op | source)
XLA Modules:
  0.0 27.9 jit_solution(6363538214037297453)
XLA Ops:
  0.6 26.1 %exchange.1 = (f32[128,512]{1,0:T(8,128)S(1)}, f32[128,512]{1,0:T(8,128)S(1)}, f32[1,128]{1,0:T(1,128)S(1)}, bf16[128,512]{1,0:T(8,128)(2,1)S(1)}, bf16[128,512]...) custom-call(bf16[128,512]{1,0:T(8,128)(2,1)} %q_hbm.1, ...), custom_call_target="tpu_custom_call" | custom-call | tf_op jit(solution)/shard_map/exchange/pallas_call | solution.py:471
  26.8 1.2 %finish.1 = (bf16[128,512]{1,0:T(8,128)(2,1)}, bf16[128,512]{1,0:T(8,128)(2,1)}, bf16[128,512]{1,0:T(8,128)(2,1)}, bf16[128,512]{1,0:T(8,128)(2,1)}, f32[1,16]{1...) custom-call(bf16[128,512]{1,0:T(8,128)(2,1)S(1)} %get-tuple-element.25.q_ref, ...), custom_call_target="tpu_custom_call" | custom-call | tf_op jit(solution)/shard_map/finish/pallas_call | solution.py:515

commit v6 on v4

--- a/solution.py
+++ b/solution.py
@@ -1,4 +1,5 @@
 import functools
+import random
 
 import jax
 import jax.numpy as jnp
@@ -13,6 +14,26 @@
 TN = (((0,), (0,)), ((), ()))
 LANES = 128
 GROUPS = 8
+
+
+MOVES = [
+    (x, y, z, core)
+    for x in range(4) for y in range(4) for z in range(4) for core in range(2)
+    if (x, y, z, core) != (0, 0, 0, 0)
+]
+
+
+def far_first(weights, ties):
+    def key(move):
+        hops = [min(step, 4 - step) for step in move[:3]]
+        return (-sum(w * h for w, h in zip(weights, hops)), ties(move))
+
+    found = {move: key(move) for move in MOVES}
+    return sorted(MOVES, key=lambda move: found[move])
+
+
+MIXED = far_first((1, 1, 1), lambda m: (m[0] * 37 + m[1] * 11 + m[2] * 23 + m[3] * 5) % 16)
+FIRST_ROUND = far_first((0.5, 1, 1.5), lambda m, draw=random.Random(0): draw.random())
 
 
 def iota(shape, axis):
@@ -49,7 +70,7 @@
     return shifted(rows, sign)
 
 
-def partners(me):
+def partners(me, moves):
     core, z = me % 2, me // 4 % 4
     y, x = me // 2 % 2 * 2 + me // 16 % 2, me // 32
     across = [lax.rem(x + d, 4) * 8 for d in range(4)]
@@ -57,12 +78,6 @@
     ups = [lax.rem(y + d, 4) for d in range(4)]
     high = [[u // 2 * 2 + lax.rem(core + d, 2) for d in range(2)] for u in ups]
     low = [lax.rem(u, 2) * 4 for u in ups]
-    moves = [
-        (dx, dy, dz, dc)
-        for dx in range(4) for dy in range(4) for dz in range(4) for dc in range(2)
-        if (dx, dy, dz, dc) != (0, 0, 0, 0)
-    ]
-    moves.sort(key=lambda m: -sum(min(d, 4 - d) for d in m[:3]))
     found = []
     for dx, dy, dz, dc in moves:
         ctx, sub = across[dx] + low[dy] + along[dz], high[dy][dc]
@@ -151,7 +166,7 @@
     slab = 2 * blocks
     modes = res_ref.shape[1]
     f32, bf16 = jnp.float32, jnp.bfloat16
-    peers = partners(me)
+    peers = partners(me, MIXED)
     barrier = pltpu.get_barrier_semaphore()
     for _, place in peers:
         pl.semaphore_signal(barrier, inc=1, device_id=place, device_id_type=MESH)
@@ -181,7 +196,7 @@
     par_buf[:, modes : 2 * modes] = res_row
 
     pl.semaphore_wait(barrier, devices - 1)
-    send_all(peers, me, out_buf, in_buf, out_send, out_recv)
+    send_all(partners(me, FIRST_ROUND), me, out_buf, in_buf, out_send, out_recv)
     send_all(peers, me, par_buf, par_all, par_send, par_recv)
     in_buf[me] = out_buf[me]
     par_all[pl.ds(me, 1), :] = par_buf[...]

time: 25.5 us -> 25.1 us (0.984)
  Pallas kernels: 24.7 us -> 24.3 us
    pallas_call x1, Pallas kernels: 23.5 us -> 23.1 us  [body(): pl.pallas_call(functools.partial(exchange_kernel, devices, sub), out_shap...]
where the time goes in v6:
time: 25.1 us; the launch traced here: 24.9 us
  Pallas kernels  24.3 us (97%)
  between operations  0.64 us (3%)
    pallas_call x1, Pallas kernels, body(): pl.pallas_call(functools.partial(exchange_kernel, devices, sub), out_shap...  23.1 us
    pallas_call x1, Pallas kernels, body(): pl.pallas_call(finish_kernel, out_shape=(wide,) * 4 + (jax.ShapeDtypeStru...  1.16 us

profile of v6, /device:TPU:1, one launch (start us, length us, event | category | flops | bytes accessed | tf_op | source)
XLA Modules:
  0.0 24.9 jit_solution(5074356985389659883)
XLA Ops:
  0.6 23.1 %exchange.1 = (f32[128,512]{1,0:T(8,128)S(1)}, f32[128,512]{1,0:T(8,128)S(1)}, f32[1,128]{1,0:T(1,128)S(1)}, bf16[128,512]{1,0:T(8,128)(2,1)S(1)}, bf16[128,512]...) custom-call(bf16[128,512]{1,0:T(8,128)(2,1)} %q_hbm.1, ...), custom_call_target="tpu_custom_call" | custom-call | tf_op jit(solution)/shard_map/exchange/pallas_call | solution.py:391
  23.8 1.2 %finish.1 = (bf16[128,512]{1,0:T(8,128)(2,1)}, bf16[128,512]{1,0:T(8,128)(2,1)}, bf16[128,512]{1,0:T(8,128)(2,1)}, bf16[128,512]{1,0:T(8,128)(2,1)}, f32[1,16]{1...) custom-call(bf16[128,512]{1,0:T(8,128)(2,1)S(1)} %get-tuple-element.25.q_ref, ...), custom_call_target="tpu_custom_call" | custom-call | tf_op jit(solution)/shard_map/finish/pallas_call | solution.py:427

commit v7 on v6

--- a/solution.py
+++ b/solution.py
@@ -34,6 +34,7 @@
 
 MIXED = far_first((1, 1, 1), lambda m: (m[0] * 37 + m[1] * 11 + m[2] * 23 + m[3] * 5) % 16)
 FIRST_ROUND = far_first((0.5, 1, 1.5), lambda m, draw=random.Random(0): draw.random())
+LAST_ROUND = far_first((1, 1, 1), lambda m, draw=random.Random(0): draw.random())
 
 
 def iota(shape, axis):
@@ -241,7 +242,7 @@
     before = running(ends, wide_speed, width, 1)
     after = running(starts, wide_speed, width, -1)
     state_buf[...] = before + after
-    send_all(peers, me, state_buf, state_all, state_send, state_recv)
+    send_all(partners(me, LAST_ROUND), me, state_buf, state_all, state_send, state_recv)
     state_all[pl.ds(me, 1), :] = state_buf[pl.ds(me, 1), :]
 
     whole(peers, par_all, par_send, par_recv).wait_recv()
@@ -283,8 +284,8 @@
     home = iota((channels, LANES), 0) % (2 * copies) - lane // modes
     for n in range(blocks):
         scaled = own_gain * jnp.exp(-own_speed * float(n * LANES))
-        factor_ref[n, :, :LANES] = jnp.where(home == 0, scaled, 0.0)
-        factor_ref[n, :, LANES:] = jnp.where(home == copies, scaled, 0.0)
+        factor_ref[n, :, :LANES] = jnp.where(home == 0, scaled, 0.0).astype(bf16)
+        factor_ref[n, :, LANES:] = jnp.where(home == copies, scaled, 0.0).astype(bf16)
     ahead = (iota((modes, LANES), 1) + 1).astype(f32)
     behind = (LANES - iota((modes, LANES), 1)).astype(f32)
     for c in range(channels):
@@ -350,8 +351,8 @@
     states = state_ref[...]
     other = pltpu.roll(states, LANES // 2, 1)
     first = iota((channels, LANES), 1) < LANES // 2
-    before = jnp.where(first, states, other)
-    after = jnp.where(first, other, states)
+    before = jnp.where(first, states, other).astype(bf16)
+    after = jnp.where(first, other, states).astype(bf16)
     for g in range(channels // tall):
         rows = slice(g * tall, (g + 1) * tall)
         deep = slice(g * tall * modes, (g + 1) * tall * modes)
@@ -362,7 +363,7 @@
             own = jnp.concatenate([found[rows, :]] * 2, axis=1)
             parts = [own * factor_ref[n, rows, :] for n in range(blocks)][::order]
             share = jnp.dot(
-                jnp.concatenate(parts, axis=0).astype(bf16),
+                jnp.concatenate(parts, axis=0),
                 table_ref[deep, :],
                 preferred_element_type=f32,
             )
@@ -385,7 +386,7 @@
     full = jax.ShapeDtypeStruct((channels, width), f32)
     square = jax.ShapeDtypeStruct((channels, LANES), f32)
     table = jax.ShapeDtypeStruct((channels * modes, LANES), bf16)
-    factors = jax.ShapeDtypeStruct((width // LANES, channels, 2 * LANES), f32)
+    factors = jax.ShapeDtypeStruct((width // LANES, channels, 2 * LANES), bf16)
     hbm = pl.BlockSpec(memory_space=pltpu.HBM)
     operands = (queries, key_branch, value_branch, out_grad, residue, log_rate, skip_gain[None, :])
     total, grad, row, q, k, v, og, *states = pl.pallas_call(

time: 25.1 us -> 24.9 us (level)
  no operation moved by 1% of the time
where the time goes in v7:
time: 24.9 us; the launch traced here: 24.8 us
  Pallas kernels  24.1 us (97%)
  between operations  0.64 us (3%)
    pallas_call x1, Pallas kernels, body(): pl.pallas_call(functools.partial(exchange_kernel, devices, sub), out_shap...  23 us
    pallas_call x1, Pallas kernels, body(): pl.pallas_call(finish_kernel, out_shape=(wide,) * 4 + (jax.ShapeDtypeStru...  1.16 us

profile of v7, /device:TPU:1, one launch (start us, length us, event | category | flops | bytes accessed | tf_op | source)
XLA Modules:
  0.0 24.8 jit_solution(15108926705421437878)
XLA Ops:
  0.6 23.0 %exchange.1 = (f32[128,512]{1,0:T(8,128)S(1)}, f32[128,512]{1,0:T(8,128)S(1)}, f32[1,128]{1,0:T(1,128)S(1)}, bf16[128,512]{1,0:T(8,128)(2,1)S(1)}, bf16[128,512]...) custom-call(bf16[128,512]{1,0:T(8,128)(2,1)} %q_hbm.1, ...), custom_call_target="tpu_custom_call" | custom-call | tf_op jit(solution)/shard_map/exchange/pallas_call | solution.py:392
  23.6 1.2 %finish.1 = (bf16[128,512]{1,0:T(8,128)(2,1)}, bf16[128,512]{1,0:T(8,128)(2,1)}, bf16[128,512]{1,0:T(8,128)(2,1)}, bf16[128,512]{1,0:T(8,128)(2,1)}, f32[1,16]{1...) custom-call(bf16[128,512]{1,0:T(8,128)(2,1)S(1)} %get-tuple-element.25.q_ref, ...), custom_call_target="tpu_custom_call" | custom-call | tf_op jit(solution)/shard_map/finish/pallas_call | solution.py:428

commit v8 on v7

--- a/solution.py
+++ b/solution.py
@@ -156,7 +156,7 @@
 def exchange_kernel(
     devices, sub, q_hbm, k_hbm, v_hbm, og_hbm, res_hbm, rate_hbm, gain_hbm,
     sum_ref, grad_ref, row_ref, q_ref, k_ref, v_ref, og_ref, state_ref, factor_ref, rise_ref,
-    fall_ref, gain_ref, res_ref, rate_ref, stage, out_buf, in_buf, par_buf, par_all, state_buf, state_all,
+    fall_ref, gain_ref, res_ref, rate_ref, stage, out_buf, in_buf, par_buf, par_all, state_buf,
     mixed_t, gated_t, conv_t, corr_t,
     load_sems, out_send, out_recv, par_send, par_recv, state_send, state_recv,
 ):
@@ -242,8 +242,8 @@
     before = running(ends, wide_speed, width, 1)
     after = running(starts, wide_speed, width, -1)
     state_buf[...] = before + after
-    send_all(partners(me, LAST_ROUND), me, state_buf, state_all, state_send, state_recv)
-    state_all[pl.ds(me, 1), :] = state_buf[pl.ds(me, 1), :]
+    send_all(partners(me, LAST_ROUND), me, state_buf, state_ref, state_send, state_recv)
+    state_ref[pl.ds(me, 1), :] = state_buf[pl.ds(me, 1), :]
 
     whole(peers, par_all, par_send, par_recv).wait_recv()
     params = par_all[...].T
@@ -330,9 +330,8 @@
 
     whole(peers, in_buf, out_send, out_recv).wait_send()
     whole(peers, par_all, par_send, par_recv).wait_send()
-    whole(peers, state_all, state_send, state_recv).wait_recv()
-    state_ref[...] = state_all[...]
-    whole(peers, state_all, state_send, state_recv).wait_send()
+    whole(peers, state_ref, state_send, state_recv).wait_recv()
+    whole(peers, state_ref, state_send, state_recv).wait_send()
 
 
 def finish_kernel(
@@ -407,7 +406,6 @@
             pltpu.VMEM((1, LANES), f32),
             pltpu.VMEM((channels, LANES), f32),
             pltpu.VMEM((devices, LANES), f32),
-            pltpu.VMEM((channels, LANES), f32),
             pltpu.VMEM((width, LANES), f32),
             pltpu.VMEM((width, LANES), f32),
             pltpu.VMEM((width, LANES), f32),

time: 24.9 us -> 24.9 us (level)
  no operation moved by 1% of the time
where the time goes in v8:
time: 24.9 us; the launch traced here: 24.8 us
  Pallas kernels  24.1 us (97%)
  between operations  0.64 us (3%)
    pallas_call x1, Pallas kernels, body(): pl.pallas_call(functools.partial(exchange_kernel, devices, sub), out_shap...  23 us
    pallas_call x1, Pallas kernels, body(): pl.pallas_call(finish_kernel, out_shape=(wide,) * 4 + (jax.ShapeDtypeStru...  1.16 us

profile of v8, /device:TPU:1, one launch (start us, length us, event | category | flops | bytes accessed | tf_op | source)
XLA Modules:
  0.0 24.8 jit_solution(3432295832829738618)
XLA Ops:
  0.6 23.0 %exchange.1 = (f32[128,512]{1,0:T(8,128)S(1)}, f32[128,512]{1,0:T(8,128)S(1)}, f32[1,128]{1,0:T(1,128)S(1)}, bf16[128,512]{1,0:T(8,128)(2,1)S(1)}, bf16[128,512]...) custom-call(bf16[128,512]{1,0:T(8,128)(2,1)} %q_hbm.1, ...), custom_call_target="tpu_custom_call" | custom-call | tf_op jit(solution)/shard_map/exchange/pallas_call | solution.py:391
  23.6 1.2 %finish.1 = (bf16[128,512]{1,0:T(8,128)(2,1)}, bf16[128,512]{1,0:T(8,128)(2,1)}, bf16[128,512]{1,0:T(8,128)(2,1)}, bf16[128,512]{1,0:T(8,128)(2,1)}, f32[1,16]{1...) custom-call(bf16[128,512]{1,0:T(8,128)(2,1)S(1)} %get-tuple-element.25.q_ref, ...), custom_call_target="tpu_custom_call" | custom-call | tf_op jit(solution)/shard_map/finish/pallas_call | solution.py:426
